TPU v7x, 256 devices: a whole 4x4x8 slice. The times are simulated.
256 devices in a mesh: rec: 8 (over y, core), tm: 32 (over x, z).
Axes of the slice: x: 4, y: 4, z: 8, core: 2. Of those that a mesh axis runs over, the one named last changes fastest.
Arguments:
- normed: bfloat16 [8, 1024, 4096], P('rec', None, 'tm'), may hold values from -6 to 6
- query_act: bfloat16 [8, 1024, 4096], P('rec', None, 'tm'), may hold values from -16 to 16
- key_act: bfloat16 [8, 1024, 4096], P('rec', None, 'tm'), may hold values from -16 to 16
- value_act: bfloat16 [8, 1024, 4096], P('rec', None, 'tm'), may hold values from -6 to 6
- grad_out: bfloat16 [8, 1024, 4096], P('rec', None, 'tm'), may hold values from -12 to 12
- w_qkv: bfloat16 [1024, 3072], replicated, may hold values from -0.1875 to 0.1875
- w_out: bfloat16 [1024, 1024], replicated, may hold values from -0.1875 to 0.1875
- lengths: int32 [8], P('rec'), may hold values from 512 to 1048576, as said below
- offsets: int32 [8], P('rec'), may hold values from 0 to 1040384
Outputs:
- grad_normed: bfloat16 [8, 1024, 4096], P('rec', None, 'tm')
- dw_qkv: float32 [1024, 3072], P('tm')
- dw_out: float32 [1024, 1024], P('tm')
Inputs may be any that keep to these rules, and one draw needn't show every extreme that they name: lengths - offsets is 512 or more for every recording, and 4096 or more for at least one recording; some recording's window ends a recording of the longest length.
All inputs are finite; a program needn't handle non-finite values.
Results may differ from a plain program's by a relative error of at most 0.035.
Values may be sent and summed in bfloat16 or wider, within the bound.
No kernel may reach another device: no remote copies, remote signals or barrier semaphores. Data moves between devices by JAX's collectives and lax.ppermute only.
A program may use at most 128 MiB of HBM per device.

v0:
```python
import math

import jax
import jax.numpy as jnp
from jax import lax
from jax.sharding import PartitionSpec as P

HEADS = 32
WINDOW = 1024
QBLOCK = 512


masked_score = -1e30


def block_terms(q_blk, g_blk, key_span, value_span, block_start, live_frames, score_scale):
    half_window = WINDOW // 2
    row_ids = block_start + jnp.arange(QBLOCK, dtype=jnp.int32)
    col_ids = block_start - half_window + jnp.arange(QBLOCK + WINDOW, dtype=jnp.int32)
    visible = (
        (col_ids[None, :] >= 0)
        & (col_ids[None, :] < live_frames)
        & (jnp.abs(row_ids[:, None] - col_ids[None, :]) < half_window)
    )
    query_live = (row_ids < live_frames).astype(jnp.float32)
    scores = (
        jnp.einsum("hdq,hdk->hqk", q_blk, key_span, preferred_element_type=jnp.float32)
        * score_scale
    )
    scores = jnp.where(visible[None], scores, masked_score)
    row_max = jnp.max(scores, axis=2, keepdims=True)
    exponent = jnp.exp(scores - row_max)
    prob = exponent / jnp.sum(exponent, axis=2, keepdims=True) * query_live[None, :, None]
    prob_b = prob.astype(jnp.bfloat16)
    attn_out = jnp.einsum(
        "hqk,hdk->hdq", prob_b, value_span, preferred_element_type=jnp.float32
    ).astype(jnp.bfloat16)
    row_dot = jnp.sum(g_blk.astype(jnp.float32) * attn_out.astype(jnp.float32), axis=1)
    prob_grad = jnp.einsum("hdq,hdk->hqk", g_blk, value_span, preferred_element_type=jnp.float32)
    dscore = (prob * (prob_grad - row_dot[:, :, None])).astype(jnp.bfloat16)
    grad_q = (
        jnp.einsum("hqk,hdk->hdq", dscore, key_span, preferred_element_type=jnp.float32)
        * score_scale
    )
    grad_k = (
        jnp.einsum("hqk,hdq->hdk", dscore, q_blk, preferred_element_type=jnp.float32) * score_scale
    )
    grad_v = jnp.einsum("hqk,hdq->hdk", prob_b, g_blk, preferred_element_type=jnp.float32)
    return (attn_out, grad_q.astype(jnp.bfloat16), grad_k, grad_v)


def window_attention(queries, key_set, values, head_grad, live_frames):
    head_count, head_dim, seq_len = queries.shape
    score_scale = 1.0 / math.sqrt(head_dim)
    half_window = WINDOW // 2
    span = QBLOCK + WINDOW
    pad_cfg = ((0, 0), (0, 0), (half_window, half_window))
    key_pad = jnp.pad(key_set, pad_cfg)
    value_pad = jnp.pad(values, pad_cfg)
    zero_acc = jnp.zeros((head_count, head_dim, seq_len + WINDOW), jnp.float32)

    def compute(operands):
        q_blk, g_blk, key_span, value_span, block_start = operands
        return block_terms(
            q_blk, g_blk, key_span, value_span, block_start, live_frames, score_scale
        )

    def step(accums, block_index):
        key_acc, value_acc = accums
        block_start = block_index * QBLOCK
        q_blk = lax.dynamic_slice_in_dim(queries, block_start, QBLOCK, 2)
        g_blk = lax.dynamic_slice_in_dim(head_grad, block_start, QBLOCK, 2)
        key_span = lax.dynamic_slice_in_dim(key_pad, block_start, span, 2)
        value_span = lax.dynamic_slice_in_dim(value_pad, block_start, span, 2)
        operands = (q_blk, g_blk, key_span, value_span, block_start)
        attn_out, grad_q, grad_k, grad_v = compute(operands)
        key_acc = lax.dynamic_update_slice_in_dim(
            key_acc,
            lax.dynamic_slice_in_dim(key_acc, block_start, span, 2) + grad_k,
            block_start,
            2,
        )
        value_acc = lax.dynamic_update_slice_in_dim(
            value_acc,
            lax.dynamic_slice_in_dim(value_acc, block_start, span, 2) + grad_v,
            block_start,
            2,
        )
        return ((key_acc, value_acc), (attn_out, grad_q))

    (key_acc, value_acc), (outs, grads) = lax.scan(
        step, (zero_acc, zero_acc), jnp.arange(seq_len // QBLOCK, dtype=jnp.int32)
    )

    def unblock(blocked):
        return jnp.transpose(blocked, (1, 2, 0, 3)).reshape(head_count, head_dim, seq_len)

    grad_key = key_acc[:, :, half_window : half_window + seq_len].astype(jnp.bfloat16)
    grad_value = value_acc[:, :, half_window : half_window + seq_len].astype(jnp.bfloat16)
    return (unblock(outs), unblock(grads), grad_key, grad_value)


def body(normed, query_act, key_act, value_act, grad_out, w_qkv, w_out, lengths, offsets):
    shards = lax.axis_size("tm")
    model_width = w_out.shape[0]
    frames = normed.shape[2]
    seq_len = frames * shards
    group_rows = model_width // shards
    head_dim = model_width // HEADS
    live_frames = jnp.clip(lengths[0] - offsets[0], 0, seq_len)
    own_input = normed[0]
    own_grad = grad_out[0]
    head_grad = lax.dot_general(
        w_out, own_grad, (((0,), (0,)), ((), ())), preferred_element_type=jnp.float32
    ).astype(jnp.bfloat16)

    def by_head(acts):
        return acts.reshape(shards, group_rows // head_dim, head_dim, frames)

    def out_terms_rows(attn_frames):

        def terms(row_start, count):
            return lax.dot_general(
                own_grad, attn_frames, (((1,), (1,)), ((), ())), preferred_element_type=jnp.float32
            )

        return terms

    attn_out, grad_query, grad_key, grad_value = window_attention(
        lax.all_to_all(by_head(query_act[0]), "tm", split_axis=0, concat_axis=3, tiled=True)[0],
        lax.all_to_all(by_head(key_act[0]), "tm", split_axis=0, concat_axis=3, tiled=True)[0],
        lax.all_to_all(by_head(value_act[0]), "tm", split_axis=0, concat_axis=3, tiled=True)[0],
        lax.all_to_all(by_head(head_grad), "tm", split_axis=0, concat_axis=3, tiled=True)[0],
        live_frames,
    )
    returned = (
        lax.all_to_all(grad_query[None], "tm", split_axis=3, concat_axis=0, tiled=True),
        lax.all_to_all(grad_key[None], "tm", split_axis=3, concat_axis=0, tiled=True),
        lax.all_to_all(grad_value[None], "tm", split_axis=3, concat_axis=0, tiled=True),
        lax.all_to_all(attn_out[None], "tm", split_axis=3, concat_axis=0, tiled=True),
    )
    pieces = tuple((piece.reshape(model_width, frames) for piece in returned[:3]))
    attn_frames = returned[3].reshape(model_width, frames)
    out_rows = out_terms_rows(attn_frames)
    blocks = [
        lax.dot_general(
            piece, own_input, (((1,), (1,)), ((), ())), preferred_element_type=jnp.float32
        )
        for piece in pieces
    ]
    blocks.append(out_rows(jnp.int32(0), group_rows * lax.axis_size("tm")))
    summed = lax.psum_scatter(
        jnp.concatenate(blocks, axis=1).astype(jnp.bfloat16), "tm", scatter_dimension=0, tiled=True
    ).astype(jnp.float32)
    qkv_part = summed[:, : 3 * model_width]
    out_part = summed[:, 3 * model_width :]
    w_three = w_qkv.reshape(model_width, 3, model_width)
    grad_total = jnp.einsum(
        "rwf,wrt->ft", w_three, jnp.stack(pieces), preferred_element_type=jnp.float32
    )
    grad_normed = grad_total.astype(jnp.bfloat16)[None]
    dw_qkv, dw_out = (
        lax.psum(qkv_part.astype(jnp.bfloat16), "rec").astype(jnp.float32),
        lax.psum(out_part.astype(jnp.bfloat16), "rec").astype(jnp.float32),
    )
    return (grad_normed, dw_qkv, dw_out)


def solution(mesh):
    return jax.shard_map(
        body,
        mesh=mesh,
        in_specs=(
            P("rec", None, "tm"),
            P("rec", None, "tm"),
            P("rec", None, "tm"),
            P("rec", None, "tm"),
            P("rec", None, "tm"),
            P(),
            P(),
            P("rec"),
            P("rec"),
        ),
        out_specs=(P("rec", None, "tm"), P("tm", None), P("tm", None)),
        check_vma=False,
    )
```

profile of v0, /device:TPU:1, one launch (start us, length us, event | category | flops | bytes accessed | tf_op | source)
XLA Modules:
  0.0 682.4 jit_solution(3352120474645500372)
XLA Ops:
  7.2 21.7 %all_to_all.120 = bf16[32,1,32,128]{3,2,1,0:T(8,128)(2,1)S(1)} all-to-all(bf16[32,1,32,128]{3,2,1,0:T(8,128)(2,1)} %bitcast.223), channel_id=1, replica_groups=mesh['rec'=8,'tm'=32] {'tm'}, dimensions={0} | all-to-all | bytes 524288 | tf_op jit(solution)/shard_map/all_to_all | solution.py:130
  28.9 6.3 all-to-all-start.1
  36.9 7.9 %all-to-all-done.1 = bf16[32,1,32,128]{3,2,1,0:T(8,128)(2,1)S(1)} async-done(((bf16[32,1,32,128]{3,2,1,0:T(8,128)(2,1)}), bf16[32,1,32,128]{3,2,1,0:T(8,128)(2,1)S(1)}, u32[]{:S(2)}, u32[]{:S(2)}) %all-to-all-start.1) | async-done | bytes 262176 | tf_op jit(solution)/shard_map/all_to_all | solution.py:131
  44.8 15.1 %all_to_all.121 = bf16[32,1,32,128]{3,2,1,0:T(8,128)(2,1)S(1)} all-to-all(bf16[32,1,32,128]{3,2,1,0:T(8,128)(2,1)S(1)} %bitcast.209), channel_id=1, replica_groups=mesh['rec'=8,'tm'=32] {'tm'}, dimensions={0} | all-to-all | bytes 524288 | tf_op jit(solution)/shard_map/all_to_all | solution.py:133
  60.0 5.2 all-to-all-start.3
  68.6 6.3 all-to-all-done.3
  76.0 102.1 %while.18 = (s32[]{:T(128)}, f32[1,32,5120]{2,1,0:T(8,128)S(1)}, f32[1,32,5120]{2,1,0:T(8,128)S(1)}, bf16[8,1,32,512]{3,2,1,0:T(8,128)(2,1)}, bf16[8,1,32,512]{3...) while((s32[]{:T(128)}, f32[1,32,5120]{2,1,0:T(8,128)S(1)}, ...), condition=%wide.region_4.5_spmd, body=%wide.region_0.4_spmd.sunk | while | flops 315629568 | bytes 28251472 | solution.py:91
  77.3 2.3 fusion.85
  86.7 2.1 fusion.91
  90.1 2.3 fusion.85
  99.5 2.1 fusion.91
  102.8 2.3 fusion.85
  112.2 2.1 fusion.91
  115.6 2.3 fusion.85
  125.0 2.1 fusion.91
  128.4 2.3 fusion.85
  137.7 2.1 fusion.91
  141.1 2.3 fusion.85
  150.5 2.1 fusion.91
  153.9 2.3 fusion.85
  163.3 2.1 fusion.91
  166.6 2.3 fusion.85
  176.0 2.1 fusion.91
  178.9 4.5 copy.96
  183.9 22.6 %reduce.14 = bf16[4096,32]{1,0:T(8,128)(2,1)S(1)} reduce(bf16[4096,1,1,32]{3,2,1,0:T(2,128)(2,1)S(1)} %bitcast.198, bf16[]{:T(256)} %broadcast.120), dimensions={1,2}, to_apply=%bitcast.142.reduce_sub_computation | reduce | bytes 524290
  208.2 4.4 all-to-all-start.6
  212.6 4.5 copy.93
  217.1 22.4 %reduce.15 = bf16[4096,32]{1,0:T(8,128)(2,1)S(1)} reduce(bf16[4096,1,1,32]{3,2,1,0:T(2,128)(2,1)S(1)} %bitcast.200, bf16[]{:T(256)} %broadcast.120), dimensions={1,2}, to_apply=%bitcast.144.reduce_sub_computation | reduce | bytes 524290
  241.3 9.6 %all-to-all-start.5 = ((bf16[32,2,2048]{2,1,0:T(2,128)(2,1)}), bf16[32,2,2048]{2,1,0:T(2,128)(2,1)}, u32[]{:S(2)}, u32[]{:S(2)}) async-start(bf16[32,2,2048]{2,1,0:T(2,128)(2,1)} %reshape.169), calls=%async_computation.5 | async-start | bytes 524288 | tf_op jit(solution)/shard_map/all_to_all | solution.py:138
  252.1 2.8 copy.90
  254.9 22.4 %reduce.16 = bf16[4096,32]{1,0:T(8,128)(2,1)S(1)} reduce(bf16[4096,1,1,32]{3,2,1,0:T(2,128)(2,1)S(1)} %bitcast.201, bf16[]{:T(256)} %broadcast.120), dimensions={1,2}, to_apply=%bitcast.146.reduce_sub_computation | reduce | bytes 524290
  279.0 9.7 %all-to-all-start.4 = ((bf16[32,2,2048]{2,1,0:T(2,128)(2,1)}), bf16[32,2,2048]{2,1,0:T(2,128)(2,1)}, u32[]{:S(2)}, u32[]{:S(2)}) async-start(bf16[32,2,2048]{2,1,0:T(2,128)(2,1)} %reshape.171), calls=%async_computation.4 | async-start | bytes 524288 | tf_op jit(solution)/shard_map/all_to_all | solution.py:137
  289.9 2.8 copy.108
  292.7 22.4 %reduce.17 = bf16[4096,32]{1,0:T(8,128)(2,1)S(1)} reduce(bf16[4096,1,1,32]{3,2,1,0:T(2,128)(2,1)S(1)} %bitcast.199, bf16[]{:T(256)} %broadcast.120), dimensions={1,2}, to_apply=%bitcast.140.reduce_sub_computation | reduce | bytes 524290
  316.8 9.3 %all-to-all-start.7 = ((bf16[32,2,2048]{2,1,0:T(2,128)(2,1)}), bf16[32,2,2048]{2,1,0:T(2,128)(2,1)S(1)}, u32[]{:S(2)}, u32[]{:S(2)}) async-start(bf16[32,2,2048]{2,1,0:T(2,128)(2,1)} %reshape.165), calls=%async_computation.7 | async-start | bytes 524288 | tf_op jit(solution)/shard_map/all_to_all | solution.py:140
  327.9 2.1 copy.97
  330.1 3.9 reshape.170
  334.0 2.1 copy.94
  336.3 3.9 reshape.172
  340.2 2.1 copy.91
  343.8 3.5 copy.109
  351.3 4.0 pad_maximum_fusion
  355.3 11.3 %copy.115 = bf16[1024,4096]{1,0:T(8,128)(2,1)} copy(bf16[1024,4096]{0,1:T(8,128)(2,1)} %pad_maximum_fusion) | data formatting | bytes 16777216
  366.7 8.6 %copy.102 = bf16[1024,3072]{0,1:T(8,128)(2,1)} copy(bf16[1024,3072]{1,0:T(8,128)(2,1)} %param.16) | data formatting | bytes 12582912 | tf_op args[5]
  375.8 223.6 %reduce-scatter.4.cloned.1.call-done = bf16[32,4096]{1,0:T(8,128)(2,1)} async-done(((bf16[1024,4096]{1,0:T(8,128)(2,1)}), bf16[32,4096]{1,0:T(8,128)(2,1)}) %reduce-scatter.4.cloned.1.call-update) | async-done | bytes 262160
  603.2 5.1 fusion.39
  609.2 62.2 %all-reduce.5.cloned.1.call-done = (bf16[32,3072]{0,1:T(8,128)(2,1)}, bf16[32,1024]{0,1:T(8,128)(2,1)}) async-done(((bf16[32,3072]{0,1:T(8,128)(2,1)}, bf16[32,1024]{0,1:T(8,128)(2,1)}), (bf16[32,3072]{0,1:T(8,128)(2,1)}, bf16[32,1024]{0,1:T(8,128)(2,1)})) %all-reduce.5.cloned.1.call-update) | async-done | bytes 262160 | tf_op jit(solution)/shard_map/psum | solution.py:163
  671.4 2.1 copy.112
  (161 shorter events, 91.6 us)
Async XLA Ops:
  7.2 28.0 %copy-start = (bf16[1024,1024]{1,0:T(8,128)(2,1)S(1)}, bf16[1024,1024]{1,0:T(8,128)(2,1)}, u32[]{:S(2)}) copy-start(bf16[1024,1024]{1,0:T(8,128)(2,1)} %param.17) | copy-start | bytes 6291460
  28.9 16.0 %all-to-all-start.1 = ((bf16[32,1,32,128]{3,2,1,0:T(8,128)(2,1)}), bf16[32,1,32,128]{3,2,1,0:T(8,128)(2,1)S(1)}, u32[]{:S(2)}, u32[]{:S(2)}) async-start(bf16[32,1,32,128]{3,2,1,0:T(8,128)(2,1)} %bitcast.224), calls=%async_computation.1 | async-start | bytes 524288 | tf_op jit(solution)/shard_map/all_to_all | solution.py:131
  60.0 14.9 %all-to-all-start.3 = ((bf16[32,1,32,128]{3,2,1,0:T(8,128)(2,1)}), bf16[32,1,32,128]{3,2,1,0:T(8,128)(2,1)S(1)}, u32[]{:S(2)}, u32[]{:S(2)}) async-start(bf16[32,1,32,128]{3,2,1,0:T(8,128)(2,1)} %bitcast.22), calls=%async_computation.3 | async-start | bytes 524288 | tf_op jit(solution)/shard_map/all_to_all | solution.py:132
  208.2 33.1 %all-to-all-start.6 = ((bf16[32,2,2048]{2,1,0:T(2,128)(2,1)}), bf16[32,2,2048]{2,1,0:T(2,128)(2,1)S(1)}, u32[]{:S(2)}, u32[]{:S(2)}) async-start(bf16[32,2,2048]{2,1,0:T(2,128)(2,1)} %reshape.167), calls=%async_computation.6 | async-start | bytes 524288 | tf_op jit(solution)/shard_map/all_to_all | solution.py:139
  241.3 37.7 %all-to-all-start.5 = ((bf16[32,2,2048]{2,1,0:T(2,128)(2,1)}), bf16[32,2,2048]{2,1,0:T(2,128)(2,1)}, u32[]{:S(2)}, u32[]{:S(2)}) async-start(bf16[32,2,2048]{2,1,0:T(2,128)(2,1)} %reshape.169), calls=%async_computation.5 | async-start | bytes 524288 | tf_op jit(solution)/shard_map/all_to_all | solution.py:138
  279.0 37.9 %all-to-all-start.4 = ((bf16[32,2,2048]{2,1,0:T(2,128)(2,1)}), bf16[32,2,2048]{2,1,0:T(2,128)(2,1)}, u32[]{:S(2)}, u32[]{:S(2)}) async-start(bf16[32,2,2048]{2,1,0:T(2,128)(2,1)} %reshape.171), calls=%async_computation.4 | async-start | bytes 524288 | tf_op jit(solution)/shard_map/all_to_all | solution.py:137
  316.8 25.6 %all-to-all-start.7 = ((bf16[32,2,2048]{2,1,0:T(2,128)(2,1)}), bf16[32,2,2048]{2,1,0:T(2,128)(2,1)S(1)}, u32[]{:S(2)}, u32[]{:S(2)}) async-start(bf16[32,2,2048]{2,1,0:T(2,128)(2,1)} %reshape.165), calls=%async_computation.7 | async-start | bytes 524288 | tf_op jit(solution)/shard_map/all_to_all | solution.py:140
  326.2 273.2 %reduce-scatter.4.cloned.1.call-start = ((), (), s32[]{:S(2)}) async-start(), calls=%async_computation.9 | async-start | bytes 8650752
  342.3 6.1 copy-start.3
  343.8 5.4 copy-start.2
  366.7 304.7 %all-reduce.5.cloned.1.call-start = ((), (), s32[]{:S(2)}) async-start(), calls=%async_computation.10 | async-start | bytes 2097152 | tf_op jit(solution)/shard_map/psum | solution.py:163
  603.2 72.0 %copy-start.1 = (bf16[1024,1024]{1,0:T(8,128)(2,1)S(1)}, bf16[1024,1024]{1,0:T(8,128)(2,1)}, u32[]{:S(2)}) copy-start(bf16[1024,1024]{1,0:T(8,128)(2,1)} %param.17) | copy-start | bytes 6291460
Sparse Core Ops, SparseCore 0:
  366.8 232.5 reduce-scatter.3
  603.3 68.0 all-reduce.4
where the time goes:
time: 691 us; the launch traced here: 682 us
  waiting for transfers between devices  300 us (43%)
  other arithmetic  105 us (15%)
  local copies, waits for them, and re-layouts  89.3 us (13%)
  matrix products  84.5 us (12%)
  starting transfers between devices  44.6 us (6%)
  blocking collectives  36.8 us (5%)
  between operations  16.1 us (2%)
    unnamed x3, waiting for transfers between devices  224 us
    unnamed x4, other arithmetic  89.8 us
    psum x1, waiting for transfers between devices, body(): lax.psum(qkv_part.astype(jnp.bfloat16), 'rec').astype(jnp.float32)  62.2 us
    unnamed x28, local copies, waits for them, and re-layouts  45.9 us
    all_to_all x1, blocking collectives, body(): lax.all_to_all(by_head(query_act[0]), 'tm', split_axis=0, concat_axis=3,...  21.7 us
    dot_general x8, matrix products, block_terms(): jnp.einsum('hdq,hdk->hqk', q_blk, key_span, preferred_element_type=jnp.fl...  18.3 us
    dot_general x8, matrix products, block_terms(): jnp.einsum('hqk,hdk->hdq', dscore, key_span, preferred_element_type=jnp.f...  16.5 us
    all_to_all x1, blocking collectives, body(): lax.all_to_all(by_head(head_grad), 'tm', split_axis=0, concat_axis=3, til...  15.1 us
  transfers between devices with their start and end apart: 8, of which 4 were waited for; matrix products, arithmetic and copies ran while one was open for 18% of the time, Pallas kernels for 0%

commit v1 on v0

v1 whole, which is shorter than its diff:
```python
import math

import jax
import jax.numpy as jnp
from jax import lax
from jax.experimental import pallas as pl
from jax.experimental.pallas import tpu as pltpu
from jax.sharding import Mesh, PartitionSpec as P

HEAD_DIM = 32
HALF = 512
QT = 256
BLK = 128
masked_score = -1e30

def attn_kernel(live_ref, x_ref, out_ref, kv_t, k_p, v_p, acc):
    blocks = x_ref.shape[0]
    seq = blocks * BLK
    span = QT + 2 * HALF
    scale = 1.0 / math.sqrt(HEAD_DIM)
    live = live_ref[0]
    f32, bf = jnp.float32, jnp.bfloat16

    zpad = jnp.zeros((HALF, BLK), bf)
    dead = jnp.where(lax.broadcasted_iota(jnp.int32, (HALF, BLK), 1) == HEAD_DIM, masked_score, 0.0).astype(bf)
    kv_t[0:HALF, :] = dead
    kv_t[HALF + seq :, :] = dead
    zl = jnp.zeros((HEAD_DIM, HALF), bf)
    for ref in (k_p, v_p):
        ref[:, 0:HALF] = zl
        ref[:, HALF + seq :] = zl
    acc[...] = jnp.zeros_like(acc)
    row_frame = lax.broadcasted_iota(jnp.int32, (HEAD_DIM, BLK), 1)
    row_id = lax.broadcasted_iota(jnp.int32, (HEAD_DIM, BLK), 0)

    def prep(b, _):
        start = pl.multiple_of(HALF + b * BLK, BLK)
        k_blk = x_ref[b, HEAD_DIM : 2 * HEAD_DIM, :]
        v_blk = x_ref[b, 2 * HEAD_DIM : 3 * HEAD_DIM, :]
        k_p[:, pl.ds(start, BLK)] = k_blk
        v_p[:, pl.ds(start, BLK)] = v_blk
        bias = jnp.where((row_id == 0) & (row_frame + b * BLK >= live), masked_score, 0.0)
        wide = jnp.concatenate(
            [k_blk.astype(f32), bias, v_blk.astype(f32), jnp.zeros((HEAD_DIM, BLK), f32)], axis=0
        )
        kv_t[pl.ds(start, BLK), :] = wide.T.astype(bf)
        return 0

    lax.fori_loop(0, blocks, prep, 0)

    b_id = lax.broadcasted_iota(jnp.int32, (QT, QT), 0)
    a_id = lax.broadcasted_iota(jnp.int32, (QT, QT), 1)
    ones_row = jnp.where(lax.broadcasted_iota(jnp.int32, (HEAD_DIM, QT), 0) == 0, 1.0, 0.0).astype(bf)
    z64 = jnp.zeros((2 * HEAD_DIM, QT), bf)
    z32 = jnp.zeros((HEAD_DIM, QT), bf)
    c = scale * math.log2(math.e)

    def dot(a, b):
        return jnp.dot(a, b, preferred_element_type=f32)

    def tile(i, _):
        base = pl.multiple_of(i * QT, QT)
        x0 = x_ref[2 * i]
        x1 = x_ref[2 * i + 1]
        q = jnp.concatenate([x0[0:32], x1[0:32]], axis=1)
        g = jnp.concatenate([x0[96:128], x1[96:128]], axis=1)
        rhs_s = jnp.concatenate([q, ones_row, z64], axis=0)
        rhs_g = jnp.concatenate([z64, g, z32], axis=0)
        kv = kv_t[pl.ds(base, span), :]
        s = dot(kv, rhs_s)
        below = b_id > a_id
        above = b_id < a_id
        edge = jnp.where(below, s[0:QT], jnp.where(above, s[span - QT :], masked_score))
        mid = s[QT : span - QT]
        m = jnp.maximum(jnp.max(mid, axis=0, keepdims=True), jnp.max(edge, axis=0, keepdims=True))
        mid = jnp.exp2((mid - m) * c)
        edge = jnp.exp2((edge - m) * c)
        total = jnp.sum(mid, axis=0, keepdims=True) + jnp.sum(edge, axis=0, keepdims=True)
        q_live = base + lax.broadcasted_iota(jnp.int32, (1, QT), 1) < live
        inv = jnp.where(q_live, 1.0 / total, 0.0)
        mid = mid * inv
        edge = edge * inv
        p = jnp.concatenate(
            [
                jnp.where(below, edge, 0.0).astype(bf),
                mid.astype(bf),
                jnp.where(above, edge, 0.0).astype(bf),
            ],
            axis=0,
        )
        ao = dot(v_p[:, pl.ds(base, span)], p).astype(bf)
        rd = jnp.sum(g.astype(f32) * ao.astype(f32), axis=0, keepdims=True)
        pg = dot(kv, rhs_g)
        d_mid = mid * (pg[QT : span - QT] - rd)
        d_edge = edge * (jnp.where(below, pg[0:QT], pg[span - QT :]) - rd)
        ds = jnp.concatenate(
            [
                jnp.where(below, d_edge, 0.0).astype(bf),
                d_mid.astype(bf),
                jnp.where(above, d_edge, 0.0).astype(bf),
            ],
            axis=0,
        )
        gq = (dot(k_p[:, pl.ds(base, span)], ds) * scale).astype(bf)
        acc[pl.ds(base, span), :] += dot(ds, rhs_s.T) + dot(p, rhs_g.T)
        for half in range(2):
            sl = slice(half * BLK, (half + 1) * BLK)
            out_ref[2 * i + half, 0:32, :] = gq[:, sl]
            out_ref[2 * i + half, 96:128, :] = ao[:, sl]
        return 0

    lax.fori_loop(0, seq // QT, tile, 0)

    def flush(b, _):
        start = pl.multiple_of(HALF + b * BLK, BLK)
        t = acc[pl.ds(start, BLK), :].T
        out_ref[b, 32:64, :] = (t[0:32] * scale).astype(bf)
        out_ref[b, 64:96, :] = t[64:96].astype(bf)
        return 0

    lax.fori_loop(0, blocks, flush, 0)

def attention(x, live):
    blocks = x.shape[0]
    seq = blocks * BLK
    padded = seq + 2 * HALF
    return pl.pallas_call(
        attn_kernel,
        out_shape=jax.ShapeDtypeStruct(x.shape, jnp.bfloat16),
        in_specs=[pl.BlockSpec(memory_space=pltpu.SMEM), pl.BlockSpec(memory_space=pltpu.VMEM)],
        out_specs=pl.BlockSpec(memory_space=pltpu.VMEM),
        scratch_shapes=[
            pltpu.VMEM((padded, BLK), jnp.bfloat16),
            pltpu.VMEM((HEAD_DIM, padded), jnp.bfloat16),
            pltpu.VMEM((HEAD_DIM, padded), jnp.bfloat16),
            pltpu.VMEM((padded, BLK), jnp.float32),
        ],
        compiler_params=pltpu.CompilerParams(vmem_limit_bytes=40 << 20),
        cost_estimate=pl.CostEstimate(flops=6 * 2 * seq * 1280 * 32, bytes_accessed=2 * x.size * 2, transcendentals=seq * 1024),
        name="window_attention",
    )(live, x)


REC_AXES = ("y", "core")
FRAME_AXES = ("x", "z")


def weight_grads(stage, normed_slice, grad_slice):
    f32, bf = jnp.float32, jnp.bfloat16
    nx, nz = stage.shape[0], stage.shape[1]
    rows = 3 * HEAD_DIM
    width = normed_slice.shape[1]
    dwq = jnp.einsum(
        "xzrt,zft->xrf", stage[:, :, :rows], normed_slice, preferred_element_type=f32
    ).astype(bf)
    dwo = jnp.einsum(
        "zct,xzdt->cxd", grad_slice, stage[:, :, rows:], preferred_element_type=f32
    ).astype(bf)
    recs = lax.axis_size(REC_AXES)
    cols = width // recs
    sub = width // (nx * nz * recs)
    send = jnp.concatenate(
        [
            dwq.reshape(nx, rows, recs, cols).transpose(2, 0, 1, 3),
            dwo.reshape(nx, nz, recs, sub, nx * HEAD_DIM)
            .transpose(2, 0, 1, 3, 4)
            .reshape(recs, nx, nz * sub, nx * HEAD_DIM),
        ],
        axis=2,
    ).reshape(recs * nx, rows + nz * sub, cols)
    terms = lax.all_to_all(send, REC_AXES + ("x",), 0, 0, tiled=True)
    summed = jnp.sum(terms.astype(f32), axis=0).astype(bf)
    out_part = lax.all_to_all(
        summed[rows:].reshape(nz, sub, nx * HEAD_DIM), "z", 0, 0, tiled=True
    ).reshape(nz * sub, nx * HEAD_DIM)
    full = lax.all_gather(jnp.concatenate([summed[:rows], out_part], axis=0), REC_AXES)
    full = full.astype(f32)
    dw_qkv = (
        full[:, :rows]
        .reshape(recs, 3, HEAD_DIM, cols)
        .transpose(2, 1, 0, 3)
        .reshape(HEAD_DIM, 3 * width)
    )
    dw_out = (
        full[:, rows:]
        .reshape(recs, nz, sub, nx, HEAD_DIM)
        .transpose(0, 2, 3, 1, 4)
        .reshape(recs * sub, width)
    )
    return dw_qkv, dw_out


def body(normed, query_act, key_act, value_act, grad_out, w_qkv, w_out, lengths, offsets):
    f32, bf = jnp.float32, jnp.bfloat16
    nx, nz = lax.axis_size("x"), lax.axis_size("z")
    shards = nx * nz
    width = w_out.shape[0]
    frames = normed.shape[2]
    seq_len = frames * shards
    live = jnp.clip(lengths - offsets, 0, seq_len).astype(jnp.int32)
    own_input = normed[0]
    own_grad = grad_out[0]
    head_grad = lax.dot_general(
        w_out, own_grad, (((0,), (0,)), ((), ())), preferred_element_type=f32
    ).astype(bf)
    sent = jnp.concatenate(
        [a.reshape(shards, HEAD_DIM, frames) for a in (query_act[0], key_act[0], value_act[0], head_grad)],
        axis=1,
    )
    heads = lax.all_to_all(sent, FRAME_AXES, 0, 0, tiled=True)
    normed_slice = lax.all_gather(own_input, "z")
    grad_slice = lax.all_gather(own_grad, "z")
    grads = attention(heads, live)
    rows = 4 * HEAD_DIM
    stage = lax.all_to_all(grads.reshape(nx, nz, rows, frames), "x", 0, 0, tiled=True)
    back = lax.all_to_all(
        stage[:, :, : 3 * HEAD_DIM].transpose(1, 0, 2, 3), "z", 0, 0, tiled=True
    )
    back = back.reshape(nz, nx, 3, HEAD_DIM, frames).transpose(2, 1, 0, 3, 4).reshape(3, width, frames)
    total = sum(
        lax.dot_general(
            w_qkv[:, i * width : (i + 1) * width],
            back[i],
            (((0,), (0,)), ((), ())),
            preferred_element_type=f32,
        )
        for i in range(3)
    )
    grad_normed = total.astype(bf)[None]
    dw_qkv, dw_out = weight_grads(stage, normed_slice, grad_slice)
    return (grad_normed, dw_qkv, dw_out)


def solution(mesh):
    chips = Mesh(mesh.devices.reshape(4, 2, 4, 8), ("y", "core", "x", "z"))
    data = P(REC_AXES, None, FRAME_AXES)
    return jax.shard_map(
        body,
        mesh=chips,
        in_specs=(data, data, data, data, data, P(), P(), P(REC_AXES), P(REC_AXES)),
        out_specs=(data, P(FRAME_AXES, None), P(FRAME_AXES, None)),
        check_vma=False,
    )
```

time: 691 us -> 202 us (0.29); the launches traced: 682 us -> 202 us
  waiting for transfers between devices: 300 us -> 58.4 us
  other arithmetic: 105 us -> 2.38 us
  local copies, waits for them, and re-layouts: 89.3 us -> 8.54 us
  matrix products: 84.5 us -> 15.1 us
  Pallas kernels: 0 us -> 37.1 us
  starting transfers between devices: 44.6 us -> 35.1 us
  blocking collectives: 36.8 us -> 29.6 us
    unnamed x3 -> x2, waiting for transfers between devices: 224 us -> 1.38 us
    unnamed x4 -> x0, other arithmetic: 89.8 us -> none
    dot_general x53 -> x5, matrix products: 82.8 us -> 13.3 us  [the longest x3 8.08 us: body(): lax.dot_general(w_qkv[:, i * width:(i + 1) * width], back[i], (((0,), (0,...]
    psum x1 -> x0, waiting for transfers between devices: 62.2 us -> none  [body(): lax.psum(qkv_part.astype(jnp.bfloat16), 'rec').astype(jnp.float32)]
    unnamed x28 -> x12, local copies, waits for them, and re-layouts: 45.9 us -> 2.53 us
    all_to_all x6 -> x4, waiting for transfers between devices: 14.2 us -> 57 us  [the longest x1 30.7 us: body(): heads = lax.all_to_all(sent, FRAME_AXES, 0, 0, tiled=True)]
    pallas_call x0 -> x1, Pallas kernels: none -> 37.1 us  [attention(): pl.pallas_call(attn_kernel, out_shape=jax.ShapeDtypeStruct(x.shape, jnp.b...]
    all_to_all x2 -> x1, blocking collectives: 36.8 us -> 14.5 us  [body(): lax.all_to_all(grads.reshape(nx, nz, rows, frames), 'x', 0, 0, tiled=True)]
  transfers between devices with their start and end apart: 8 -> 6, of which waited for: 4 -> 4; matrix products, arithmetic and copies ran while one was open for 18% -> 11% of each run, Pallas kernels for 0% -> 18%
where the time goes in v1:
time: 202 us
  waiting for transfers between devices  58.4 us (29%)
  Pallas kernels  37.1 us (18%)
  starting transfers between devices  35.1 us (17%)
  blocking collectives  29.6 us (15%)
  between operations  15.6 us (8%)
  matrix products  15.1 us (7%)
  local copies, waits for them, and re-layouts  8.54 us (4%)
  other arithmetic  2.38 us (1%)
    pallas_call x1, Pallas kernels, attention(): pl.pallas_call(attn_kernel, out_shape=jax.ShapeDtypeStruct(x.shape, jnp.b...  37.1 us
    all_to_all x1, waiting for transfers between devices, body(): heads = lax.all_to_all(sent, FRAME_AXES, 0, 0, tiled=True)  30.7 us
    all_gather x1, blocking collectives, weight_grads(): lax.all_gather(jnp.concatenate([summed[:rows], out_part], axis=0), REC_AXES)  15.1 us
    all_to_all x1, blocking collectives, body(): lax.all_to_all(grads.reshape(nx, nz, rows, frames), 'x', 0, 0, tiled=True)  14.5 us
    all_to_all x1, waiting for transfers between devices, body(): lax.all_to_all(stage[:, :, :3 * HEAD_DIM].transpose(1, 0, 2, 3), 'z', 0,...  13.9 us
    all_to_all x1, starting transfers between devices, body(): lax.all_to_all(stage[:, :, :3 * HEAD_DIM].transpose(1, 0, 2, 3), 'z', 0,...  12.1 us
    all_to_all x1, starting transfers between devices, body(): heads = lax.all_to_all(sent, FRAME_AXES, 0, 0, tiled=True)  11.9 us
    all_to_all x1, waiting for transfers between devices, weight_grads(): terms = lax.all_to_all(send, REC_AXES + ('x',), 0, 0, tiled=True)  8.97 us
  transfers between devices with their start and end apart: 6, of which 4 were waited for; matrix products, arithmetic and copies ran while one was open for 11% of the time, Pallas kernels for 18%

profile of v1, /device:TPU:1, one launch (start us, length us, event | category | flops | bytes accessed | tf_op | source)
XLA Modules:
  0.0 201.7 jit_solution(3883480468872187640)
XLA Ops:
  7.2 0.0 copy-start
  7.2 0.0 all-gather.6.cloned.1.call-start
  7.2 0.7 all-gather.6.cloned.1.call-update
  7.9 0.8 copy-done
  8.8 0.0 copy-start.2
  8.8 0.0 copy-start.3
  8.8 1.8 convolution_convert_fusion
  10.6 0.0 copy-done.2
  10.6 0.0 copy-done.3
  10.6 0.0 copy-done.4
  10.6 1.1 pad_maximum_fusion
  11.7 11.9 %all-to-all-start = ((bf16[32,128,128]{2,1,0:T(8,128)(2,1)}), bf16[32,128,128]{2,1,0:T(8,128)(2,1)S(1)}, u32[]{:S(2)}, u32[]{:S(2)}) async-start(bf16[32,128,128]{2,1,0:T(8,128)(2,1)} %pad_maximum_fusion), calls=%async_computation | async-start | bytes 2097152 | tf_op jit(solution)/shard_map/all_to_all | solution.py:210
  23.6 0.0 all-gather.4.cloned.1.call-start
  23.6 0.7 all-gather.4.cloned.1.call-update
  25.6 30.7 %all-to-all-done.x_ref = bf16[32,128,128]{2,1,0:T(8,128)(2,1)S(1)} async-done(((bf16[32,128,128]{2,1,0:T(8,128)(2,1)}), bf16[32,128,128]{2,1,0:T(8,128)(2,1)S(1)}, u32[]{:S(2)}, u32[]{:S(2)}) %all-to-all-start) | async-done | bytes 1048608 | tf_op jit(solution)/shard_map/all_to_all | solution.py:210
  56.3 37.1 %window_attention.1 = bf16[32,128,128]{2,1,0:T(8,128)(2,1)S(1)} custom-call(s32[1]{0:T(128)S(6)} %min.6.live_ref, bf16[32,128,128]{2,1,0:T(8,128)(2,1)S(1)} %all-to-all-done.x_ref), custom_call_target="tpu_custom_call" | custom-call | flops 2013265920 | bytes 2097152 | tf_op jit(solution)/shard_map/window_attention/pallas_call | solution.py:127
  93.4 14.5 %all_to_all.25 = bf16[4,8,128,128]{3,2,1,0:T(8,128)(2,1)S(1)} all-to-all(bf16[4,8,128,128]{3,2,1,0:T(8,128)(2,1)S(1)} %bitcast.79), channel_id=1, replica_groups=mesh['y'=4,'core'=2,'x'=4,'z'=8] {'x'}, dimensions={0} | all-to-all | bytes 2097152 | tf_op jit(solution)/shard_map/all_to_all | solution.py:215
  107.9 0.1 slice_bitcast_fusion
  108.0 1.1 copy.37
  109.0 12.1 %all-to-all-start.2 = ((bf16[8,4,96,128]{3,2,1,0:T(8,128)(2,1)}), bf16[8,4,96,128]{3,2,1,0:T(8,128)(2,1)}, u32[]{:S(2)}, u32[]{:S(2)}) async-start(bf16[8,4,96,128]{3,2,1,0:T(8,128)(2,1)} %copy.37), calls=%async_computation.2 | async-start | bytes 1572864 | tf_op jit(solution)/shard_map/all_to_all | solution.py:216
  121.2 0.0 all-gather.6.cloned.1.call-done
  121.2 0.0 copy-done.1
  121.2 2.4 %fusion.30 = bf16[1024,4,32]{0,2,1:T(8,128)(2,1)S(1)} fusion(bf16[8,1024,128]{2,1,0:T(8,128)(2,1)} %all-gather.6.cloned.1.call-done, bf16[4,8,128,128]{3,2,1,0:T(8,128)(2,1)S(1)} %all_to_all.25), kind=kOutput, calls=%fused_computation.18 | convolution fusion | flops 268566528 | bytes 2621440 | tf_op jit(solution)/shard_map/zct,xzdt->cxd/dot_general | solution.py:156
  123.6 0.7 copy.42
  124.3 0.5 reshape.55
  124.8 0.1 copy.43
  124.9 0.0 all-gather.4.cloned.1.call-done
  125.0 2.9 %fusion.12 = bf16[4,12,8,8,128]{4,3,2,1,0:T(8,128)(2,1)S(1)} fusion(bf16[8,1024,128]{2,1,0:T(8,128)(2,1)} %all-gather.4.cloned.1.call-done, bf16[4,8,128,128]{3,2,1,0:T(8,128)(2,1)} %copy-done.1), kind=kOutput, calls=%fused_computation.11 | convolution fusion | flops 805699584 | bytes 3670016 | tf_op jit(solution)/shard_map/xzrt,zft->xrf/dot_general | solution.py:153
  127.8 0.1 copy.53
  128.0 1.1 pad_maximum_fusion.1
  129.1 13.9 %all-to-all-done.2 = bf16[8,4,96,128]{3,2,1,0:T(8,128)(2,1)} async-done(((bf16[8,4,96,128]{3,2,1,0:T(8,128)(2,1)}), bf16[8,4,96,128]{3,2,1,0:T(8,128)(2,1)}, u32[]{:S(2)}, u32[]{:S(2)}) %all-to-all-start.2) | async-done | bytes 786464 | tf_op jit(solution)/shard_map/all_to_all | solution.py:216
  143.1 7.6 %all-to-all-start.3 = ((bf16[32,128,128]{2,1,0:T(8,128)(2,1)}), bf16[32,128,128]{2,1,0:T(8,128)(2,1)S(1)}, u32[]{:S(2)}, u32[]{:S(2)}) async-start(bf16[32,128,128]{2,1,0:T(8,128)(2,1)} %pad_maximum_fusion.1), calls=%async_computation.3 | async-start | bytes 2097152 | tf_op jit(solution)/shard_map/all_to_all | solution.py:171
  150.7 1.2 fusion.39
  152.0 2.9 %fusion.4 = f32[128,1024]{1,0:T(8,128)} fusion(bf16[1024,128]{1,0:T(8,128)(2,1)S(1)} %bitcast.90, bf16[1024,3072]{1,0:T(8,128)(2,1)} %param.14), kind=kOutput, calls=%fused_computation.4 | convolution fusion | flops 268435456 | bytes 2883584 | tf_op jit(solution)/shard_map/dot_general | solution.py:221
  154.9 2.9 %fusion.6 = f32[128,1024]{1,0:T(8,128)} fusion(bf16[1024,128]{1,0:T(8,128)(2,1)S(1)} %bitcast.91, bf16[1024,3072]{1,0:T(8,128)(2,1)} %param.14), kind=kOutput, calls=%fused_computation.6 | convolution fusion | flops 268435456 | bytes 2883584 | tf_op jit(solution)/shard_map/dot_general | solution.py:221
  157.8 9.0 %all-to-all-done.3 = bf16[32,128,128]{2,1,0:T(8,128)(2,1)S(1)} async-done(((bf16[32,128,128]{2,1,0:T(8,128)(2,1)}), bf16[32,128,128]{2,1,0:T(8,128)(2,1)S(1)}, u32[]{:S(2)}, u32[]{:S(2)}) %all-to-all-start.3) | async-done | bytes 1048608 | tf_op jit(solution)/shard_map/all_to_all | solution.py:171
  166.7 0.2 reduce_sum.12
  166.9 0.6 slice.58
  167.5 3.3 %all-to-all-start.4 = ((bf16[8,4,128]{2,1,0:T(4,128)(2,1)}), bf16[8,4,128]{2,1,0:T(4,128)(2,1)S(1)}, u32[]{:S(2)}, u32[]{:S(2)}) async-start(bf16[8,4,128]{2,1,0:T(4,128)(2,1)} %bitcast.26), calls=%async_computation.4 | async-start | bytes 16384 | tf_op jit(solution)/shard_map/all_to_all | solution.py:173
  170.8 2.3 %fusion.33 = bf16[1,1024,128]{1,2,0:T(8,128)(2,1)S(1)} fusion(f32[128,1024]{1,0:T(8,128)} %fusion.4, f32[128,1024]{1,0:T(8,128)} %fusion.6, bf16[1024,128]{1,0:T(8,128)(2,1)S(1)} %bitcast.87, bf16[1024,3072]{1,0:T(8,128)(2,1)} %param.14), kind=kOutput, calls=%fused_computation.19 | convolution fusion | flops 268828672 | bytes 3670016 | tf_op jit(solution)/shard_map/dot_general | solution.py:221
  173.1 0.8 copy.46
  174.0 3.4 %all-to-all-done.4 = bf16[8,4,128]{2,1,0:T(4,128)(2,1)S(1)} async-done(((bf16[8,4,128]{2,1,0:T(4,128)(2,1)}), bf16[8,4,128]{2,1,0:T(4,128)(2,1)S(1)}, u32[]{:S(2)}, u32[]{:S(2)}) %all-to-all-start.4) | async-done | bytes 8224 | tf_op jit(solution)/shard_map/all_to_all | solution.py:173
  177.3 15.1 %all-gather = bf16[1024,128]{1,0:T(8,128)(2,1)S(1)} all-gather(bf16[128,128]{1,0:T(8,128)(2,1)S(1)} %pad_maximum_fusion.2), channel_id=2, replica_groups=mesh['y'=4,'core'=2,'x'=4,'z'=8] {'y','core'}, dimensions={0}, use_global_device_ids=true | all-gather | bytes 294912 | tf_op jit(solution)/shard_map/all_gather | solution.py:176
  192.5 0.3 reshape.60
  192.7 0.2 copy.45
  192.9 0.9 reshape.61
  193.8 0.2 copy.44
  194.0 0.8 copy.54
  (9 shorter events, 0.1 us)
Async XLA Ops:
  7.2 1.6 copy-start
  7.2 114.0 %all-gather.6.cloned.1.call-start = ((), (), s32[]{:S(2)}) async-start(), calls=%async_computation.6 | async-start | bytes 2359296 | tf_op jit(solution)/shard_map/all_gather | solution.py:212
  8.8 1.8 copy-start.2
  8.8 1.8 copy-start.3
  8.8 1.8 copy-start.4
  11.7 44.6 %all-to-all-start = ((bf16[32,128,128]{2,1,0:T(8,128)(2,1)}), bf16[32,128,128]{2,1,0:T(8,128)(2,1)S(1)}, u32[]{:S(2)}, u32[]{:S(2)}) async-start(bf16[32,128,128]{2,1,0:T(8,128)(2,1)} %pad_maximum_fusion), calls=%async_computation | async-start | bytes 2097152 | tf_op jit(solution)/shard_map/all_to_all | solution.py:210
  23.6 101.4 %all-gather.4.cloned.1.call-start = ((), (), s32[]{:S(2)}) async-start(), calls=%async_computation.5 | async-start | bytes 2359296 | tf_op jit(solution)/shard_map/all_gather | solution.py:211
  107.9 13.3 %copy-start.1 = (bf16[4,8,128,128]{3,2,1,0:T(8,128)(2,1)}, bf16[4,8,128,128]{3,2,1,0:T(8,128)(2,1)S(1)}, u32[]{:S(2)}) copy-start(bf16[4,8,128,128]{3,2,1,0:T(8,128)(2,1)S(1)} %all_to_all.25) | copy-start | bytes 3145732
  109.0 34.0 %all-to-all-start.2 = ((bf16[8,4,96,128]{3,2,1,0:T(8,128)(2,1)}), bf16[8,4,96,128]{3,2,1,0:T(8,128)(2,1)}, u32[]{:S(2)}, u32[]{:S(2)}) async-start(bf16[8,4,96,128]{3,2,1,0:T(8,128)(2,1)} %copy.37), calls=%async_computation.2 | async-start | bytes 1572864 | tf_op jit(solution)/shard_map/all_to_all | solution.py:216
  143.1 23.7 %all-to-all-start.3 = ((bf16[32,128,128]{2,1,0:T(8,128)(2,1)}), bf16[32,128,128]{2,1,0:T(8,128)(2,1)S(1)}, u32[]{:S(2)}, u32[]{:S(2)}) async-start(bf16[32,128,128]{2,1,0:T(8,128)(2,1)} %pad_maximum_fusion.1), calls=%async_computation.3 | async-start | bytes 2097152 | tf_op jit(solution)/shard_map/all_to_all | solution.py:171
  167.5 9.9 %all-to-all-start.4 = ((bf16[8,4,128]{2,1,0:T(4,128)(2,1)}), bf16[8,4,128]{2,1,0:T(4,128)(2,1)S(1)}, u32[]{:S(2)}, u32[]{:S(2)}) async-start(bf16[8,4,128]{2,1,0:T(4,128)(2,1)} %bitcast.26), calls=%async_computation.4 | async-start | bytes 16384 | tf_op jit(solution)/shard_map/all_to_all | solution.py:173
Sparse Core Ops, SparseCore 0:
  9.8 61.6 all-gather.5
  73.3 37.2 all-gather.3

commit v2 on v1

v2 whole, which is shorter than its diff:
```python
import math

import jax
import jax.numpy as jnp
from jax import lax
from jax.experimental import pallas as pl
from jax.experimental.pallas import tpu as pltpu
from jax.sharding import Mesh, PartitionSpec as P

HEAD_DIM = 32
HALF = 512
QT = 256
BLK = 128
GROUP = 4
UNROLL = 16
masked_score = -1e30
REC_AXES = ("y", "core")
FRAME_AXES = ("x", "z")
NT = (((1,), (1,)), ((), ()))


def attn_kernel(ids_ref, x_ref, out_ref, kv_t, k_p, v_p, acc):
    blocks = x_ref.shape[0]
    seq = blocks * BLK
    span = QT + 2 * HALF
    scale = 1.0 / math.sqrt(HEAD_DIM)
    live = ids_ref[0]
    f32, bf = jnp.float32, jnp.bfloat16

    zpad = jnp.zeros((HALF, BLK), bf)
    dead = jnp.where(lax.broadcasted_iota(jnp.int32, (HALF, BLK), 1) == HEAD_DIM, masked_score, 0.0).astype(bf)
    kv_t[0:HALF, :] = dead
    kv_t[HALF + seq :, :] = dead
    zl = jnp.zeros((HEAD_DIM, HALF), bf)
    for ref in (k_p, v_p):
        ref[:, 0:HALF] = zl
        ref[:, HALF + seq :] = zl
    acc[...] = jnp.zeros_like(acc)
    row_frame = lax.broadcasted_iota(jnp.int32, (HEAD_DIM, BLK), 1)
    row_id = lax.broadcasted_iota(jnp.int32, (HEAD_DIM, BLK), 0)

    def prep(b, _):
        start = pl.multiple_of(HALF + b * BLK, BLK)
        k_blk = x_ref[b, HEAD_DIM : 2 * HEAD_DIM, :]
        v_blk = x_ref[b, 2 * HEAD_DIM : 3 * HEAD_DIM, :]
        k_p[:, pl.ds(start, BLK)] = k_blk
        v_p[:, pl.ds(start, BLK)] = v_blk
        bias = jnp.where((row_id == 0) & (row_frame + b * BLK >= live), masked_score, 0.0)
        wide = jnp.concatenate(
            [k_blk.astype(f32), bias, v_blk.astype(f32), jnp.zeros((HEAD_DIM, BLK), f32)], axis=0
        )
        kv_t[pl.ds(start, BLK), :] = wide.T.astype(bf)
        return 0

    lax.fori_loop(0, blocks, prep, 0, unroll=UNROLL)

    b_id = lax.broadcasted_iota(jnp.int32, (QT, QT), 0)
    a_id = lax.broadcasted_iota(jnp.int32, (QT, QT), 1)
    ones_row = jnp.where(lax.broadcasted_iota(jnp.int32, (HEAD_DIM, QT), 0) == 0, 1.0, 0.0).astype(bf)
    z64 = jnp.zeros((2 * HEAD_DIM, QT), bf)
    z32 = jnp.zeros((HEAD_DIM, QT), bf)
    c = scale * math.log2(math.e)

    def dot(a, b):
        return jnp.dot(a, b, preferred_element_type=f32)

    below = b_id > a_id
    above = b_id < a_id

    def group(n, _):
        tiles = [n * GROUP + j for j in range(GROUP)]
        bases = [pl.multiple_of(i * QT, QT) for i in tiles]
        qs, gs = [], []
        for i in tiles:
            x0, x1 = x_ref[2 * i], x_ref[2 * i + 1]
            q = jnp.concatenate([x0[0:32], x1[0:32]], axis=1)
            g = jnp.concatenate([x0[96:128], x1[96:128]], axis=1)
            qs.append(jnp.concatenate([q, ones_row, z64], axis=0))
            gs.append(jnp.concatenate([z64, g, z32], axis=0))
        kvs = [kv_t[pl.ds(b, span), :] for b in bases]
        ss = [dot(kv, r) for kv, r in zip(kvs, qs)]
        pgs = [dot(kv, r) for kv, r in zip(kvs, gs)]
        mids, edges, ps, aos = [], [], [], []
        for j in range(GROUP):
            s = ss[j]
            edge = jnp.where(below, s[0:QT], jnp.where(above, s[span - QT :], masked_score))
            mid = s[QT : span - QT]
            m = jnp.maximum(jnp.max(mid, axis=0, keepdims=True), jnp.max(edge, axis=0, keepdims=True))
            mid = jnp.exp2((mid - m) * c)
            edge = jnp.exp2((edge - m) * c)
            total = jnp.sum(mid, axis=0, keepdims=True) + jnp.sum(edge, axis=0, keepdims=True)
            q_live = bases[j] + lax.broadcasted_iota(jnp.int32, (1, QT), 1) < live
            inv = jnp.where(q_live, 1.0 / total, 0.0)
            mid = mid * inv
            edge = edge * inv
            p = jnp.concatenate(
                [jnp.where(below, edge, 0.0).astype(bf), mid.astype(bf), jnp.where(above, edge, 0.0).astype(bf)],
                axis=0,
            )
            mids.append(mid)
            edges.append(edge)
            ps.append(p)
            aos.append(dot(v_p[:, pl.ds(bases[j], span)], p).astype(bf))
        dss, gqs = [], []
        for j in range(GROUP):
            pg = pgs[j]
            rd = jnp.sum(gs[j][64:96].astype(f32) * aos[j].astype(f32), axis=0, keepdims=True)
            d_mid = mids[j] * (pg[QT : span - QT] - rd)
            d_edge = edges[j] * (jnp.where(below, pg[0:QT], pg[span - QT :]) - rd)
            ds = jnp.concatenate(
                [jnp.where(below, d_edge, 0.0).astype(bf), d_mid.astype(bf), jnp.where(above, d_edge, 0.0).astype(bf)],
                axis=0,
            )
            dss.append(ds)
            gqs.append((dot(k_p[:, pl.ds(bases[j], span)], ds) * scale).astype(bf))
        for j in range(GROUP):
            acc[pl.ds(bases[j], span), :] += dot(dss[j], qs[j].T) + dot(ps[j], gs[j].T)
        for j in range(GROUP):
            for half in range(2):
                sl = slice(half * BLK, (half + 1) * BLK)
                out_ref[2 * tiles[j] + half, 0:32, :] = gqs[j][:, sl]
                out_ref[2 * tiles[j] + half, 96:128, :] = aos[j][:, sl]
        return 0

    lax.fori_loop(0, seq // QT // GROUP, group, 0)

    def flush(b, _):
        start = pl.multiple_of(HALF + b * BLK, BLK)
        t = acc[pl.ds(start, BLK), :].T
        out_ref[b, 32:64, :] = (t[0:32] * scale).astype(bf)
        out_ref[b, 64:96, :] = t[64:96].astype(bf)
        return 0

    lax.fori_loop(0, blocks, flush, 0, unroll=UNROLL)

def attention(x, ids):
    blocks = x.shape[0]
    seq = blocks * BLK
    padded = seq + 2 * HALF
    return pl.pallas_call(
        attn_kernel,
        out_shape=jax.ShapeDtypeStruct(x.shape, jnp.bfloat16),
        in_specs=[pl.BlockSpec(memory_space=pltpu.SMEM), pl.BlockSpec(memory_space=pltpu.VMEM)],
        out_specs=pl.BlockSpec(memory_space=pltpu.VMEM),
        scratch_shapes=[
            pltpu.VMEM((padded, BLK), jnp.bfloat16),
            pltpu.VMEM((HEAD_DIM, padded), jnp.bfloat16),
            pltpu.VMEM((HEAD_DIM, padded), jnp.bfloat16),
            pltpu.VMEM((padded, BLK), jnp.float32),
        ],
        compiler_params=pltpu.CompilerParams(vmem_limit_bytes=40 << 20),
        cost_estimate=pl.CostEstimate(
            flops=6 * 2 * seq * (QT + 2 * HALF) * HEAD_DIM, bytes_accessed=2 * x.size * 2, transcendentals=seq * 2 * HALF
        ),
        name="window_attention",
    )(ids, x)


def terms_kernel(ids_ref, stage_ref, gathered_ref, out_ref):
    own_x, own_core = ids_ref[1], ids_ref[2]
    nx, nz, rows, frames = stage_ref.shape
    width = gathered_ref.shape[1] // 2
    g_rows = 3 * HEAD_DIM
    f32, bf = jnp.float32, jnp.bfloat16

    def wide(ref_slice):
        return [
            jnp.concatenate([ref_slice(k), ref_slice(k + 1)], axis=1) for k in range(0, nz, 2)
        ]

    def product(lefts, rights):
        return sum(
            lax.dot_general(a, b, NT, preferred_element_type=f32) for a, b in zip(lefts, rights)
        )

    grads = wide(lambda k: stage_ref[:, k, :g_rows, :].reshape(nx * g_rows, frames))
    aos = wide(lambda k: stage_ref[:, k, g_rows:, :].reshape(nx * HEAD_DIM, frames))
    half = width // 2
    blocks = half // BLK
    for core in range(2):
        slot = lax.rem(core + own_core, 2)
        for pair in range(blocks // 2):
            start = core * half + pair * 2 * BLK
            total = product(grads, wide(lambda k: gathered_ref[k, start : start + 2 * BLK, :]))
            total = total.astype(bf).reshape(nx, g_rows, 2 * BLK)
            for x in range(nx):
                to = lax.rem(x - own_x + nx, nx)
                for j in range(2):
                    b = 2 * pair + j
                    out_ref[slot, to, b * g_rows : (b + 1) * g_rows, :] = total[
                        x, :, j * BLK : (j + 1) * BLK
                    ]
    per_x = width // nx
    sub = HEAD_DIM // 2
    for x in range(nx):
        to = lax.rem(x - own_x + nx, nx)
        start = width + x * per_x
        total = product(wide(lambda k: gathered_ref[k, start : start + per_x, :]), aos)
        total = total.astype(bf).reshape(nz, 2, sub, nx * HEAD_DIM)
        for core in range(2):
            out_ref[lax.rem(core + own_core, 2), to, blocks * g_rows :, :] = total[
                :, core
            ].reshape(nz * sub, nx * HEAD_DIM)


def input_grad_kernel(w_ref, back_ref, out_ref, buf):
    nz, nx = back_ref.shape[:2]
    width = w_ref.shape[0]
    for z in range(nz):
        for x in range(nx):
            start = (x * nz + z) * HEAD_DIM
            for i in range(3):
                buf[i, start : start + HEAD_DIM, :] = back_ref[
                    z, x, i * HEAD_DIM : (i + 1) * HEAD_DIM, :
                ]
    total = jnp.zeros((BLK, width), jnp.float32)
    for i in range(3):
        total += jnp.dot(
            buf[i].T, w_ref[:, i * width : (i + 1) * width], preferred_element_type=jnp.float32
        )
    out_ref[...] = total.T.astype(jnp.bfloat16)


def local_call(kernel, name, out_shape, flops, scratch, *args):
    size = sum(a.size * a.dtype.itemsize for a in args) + math.prod(out_shape) * 2
    spaces = [pltpu.SMEM if a.dtype == jnp.int32 else pltpu.VMEM for a in args]
    return pl.pallas_call(
        kernel,
        out_shape=jax.ShapeDtypeStruct(out_shape, jnp.bfloat16),
        in_specs=[pl.BlockSpec(memory_space=space) for space in spaces],
        out_specs=pl.BlockSpec(memory_space=pltpu.VMEM),
        scratch_shapes=scratch,
        compiler_params=pltpu.CompilerParams(vmem_limit_bytes=40 << 20),
        cost_estimate=pl.CostEstimate(flops=flops, bytes_accessed=size, transcendentals=0),
        name=name,
    )(*args)


def swap_cores(v):
    return lax.ppermute(v, "core", [(0, 1), (1, 0)])


def shift(v, axis, k):
    n = lax.axis_size(axis)
    return lax.ppermute(v, axis, [(i, (i + k) % n) for i in range(n)])


def add_up(*terms):
    terms = [t.astype(jnp.float32) for t in terms]
    while len(terms) > 1:
        terms = [a + b for a, b in zip(terms[::2], terms[1::2])]
    return terms[0].astype(jnp.bfloat16)


def weight_grads(terms, back, width):
    nz = lax.axis_size("z")
    core = lax.axis_index("core")
    mine = add_up(terms[0], swap_cores(terms[1]))
    mine = add_up(mine[0], shift(mine[2], "x", 2), shift(mine[1], "x", 1), shift(mine[3], "x", 3))
    mine = add_up(mine, shift(mine, "y", 2), shift(mine, "y", 1), shift(mine, "y", 3))
    g_rows = 3 * HEAD_DIM
    blocks = width // 2 // BLK
    sub = HEAD_DIM // 2

    def both(part):
        other = swap_cores(part)
        return jnp.where(core == 0, jnp.stack([part, other]), jnp.stack([other, part]))

    qkv = both(mine[: blocks * g_rows]).reshape(2, blocks, 3, HEAD_DIM, BLK)
    dw_qkv = qkv.transpose(3, 2, 0, 1, 4).reshape(HEAD_DIM, 3 * width).astype(jnp.float32)
    out = mine[blocks * g_rows :].reshape(nz, sub, BLK)
    out, back = lax.optimization_barrier((out, back))
    out = both(lax.all_to_all(out, "z", 0, 0, tiled=True))
    out = out.reshape(2, nz, sub, BLK // HEAD_DIM, HEAD_DIM)
    dw_out = out.transpose(0, 2, 3, 1, 4).reshape(2 * sub, width).astype(jnp.float32)
    return dw_qkv, dw_out, back


def body(normed, query_act, key_act, value_act, grad_out, w_qkv, w_out, lengths, offsets):
    f32, bf = jnp.float32, jnp.bfloat16
    nx, nz = lax.axis_size("x"), lax.axis_size("z")
    shards = nx * nz
    width = w_out.shape[0]
    frames = normed.shape[2]
    seq_len = frames * shards
    rows = 4 * HEAD_DIM
    live = jnp.clip(lengths[0] - offsets[0], 0, seq_len)
    ids = jnp.stack([live, lax.axis_index("x"), lax.axis_index("core")]).astype(jnp.int32)
    own_grad = grad_out[0]
    gathered = lax.all_gather(jnp.concatenate([normed[0], own_grad], axis=0), "z")
    head_grad = lax.dot_general(
        w_out, own_grad, (((0,), (0,)), ((), ())), preferred_element_type=f32
    ).astype(bf)
    sent = jnp.concatenate(
        [a.reshape(shards, HEAD_DIM, frames) for a in (query_act[0], key_act[0], value_act[0], head_grad)],
        axis=1,
    )
    heads = lax.all_to_all(sent, FRAME_AXES, 0, 0, tiled=True)
    grads = attention(heads, ids)

    stage = lax.all_to_all(grads.reshape(nx, nz, rows, frames), "x", 0, 0, tiled=True)
    back = lax.all_to_all(
        stage[:, :, : 3 * HEAD_DIM].transpose(1, 0, 2, 3), "z", 0, 0, tiled=True
    )
    terms = local_call(
        terms_kernel,
        "weight_grad_terms",
        (2, nx, width // 2 // BLK * 3 * HEAD_DIM + nz * HEAD_DIM // 2, BLK),
        2 * nx * rows * width * nz * frames,
        [],
        ids,
        stage,
        gathered,
    )
    dw_qkv, dw_out, back = weight_grads(terms, back, width)
    grad_normed = local_call(
        input_grad_kernel,
        "input_grad",
        (width, frames),
        6 * width * width * frames,
        [pltpu.VMEM((3, width, frames), bf)],
        w_qkv,
        back,
    )[None]
    return (grad_normed, dw_qkv, dw_out)


def solution(mesh):
    chips = Mesh(mesh.devices.reshape(4, 2, 4, 8), ("y", "core", "x", "z"))
    data = P(REC_AXES, None, FRAME_AXES)
    return jax.shard_map(
        body,
        mesh=chips,
        in_specs=(data, data, data, data, data, P(), P(), P(REC_AXES), P(REC_AXES)),
        out_specs=(data, P(FRAME_AXES, None), P(FRAME_AXES, None)),
        check_vma=False,
    )
```

time: 202 us -> 165 us (0.82)
  blocking collectives: 29.6 us -> 15.8 us
  matrix products: 15.1 us -> 1.78 us
  Pallas kernels: 37.1 us -> 23.9 us
  waiting for transfers between devices: 58.4 us -> 51.9 us
  starting transfers between devices: 35.1 us -> 39.9 us
  other arithmetic: 2.38 us -> 4.83 us
  local copies, waits for them, and re-layouts: 8.54 us -> 10.9 us
    ppermute x0 -> x9, starting transfers between devices: none -> 17.5 us  [the longest x6 9.07 us: shift(): return lax.ppermute(v, axis, [(i, (i + k) % n) for i in range(n)])]
    pallas_call x1, Pallas kernels: 37.1 us -> 20 us  [attention(): pl.pallas_call(attn_kernel, out_shape=jax.ShapeDtypeStruct(x.shape, jnp.b...]
    all_gather x1 -> x0, blocking collectives: 15.1 us -> none  [weight_grads(): lax.all_gather(jnp.concatenate([summed[:rows], out_part], axis=0), REC_AXES)]
    dot_general x5 -> x0, matrix products: 13.3 us -> none  [the longest x3 8.08 us: body(): lax.dot_general(w_qkv[:, i * width:(i + 1) * width], back[i], (((0,), (0,...]
    all_to_all x1, waiting for transfers between devices: 13.9 us -> 1.98 us  [body(): lax.all_to_all(stage[:, :, :3 * HEAD_DIM].transpose(1, 0, 2, 3), 'z', 0,...]
    ppermute x0 -> x9, waiting for transfers between devices: none -> 10.4 us  [the longest x6 10.4 us: shift(): return lax.ppermute(v, axis, [(i, (i + k) % n) for i in range(n)])]
    all_to_all x2 -> x1, waiting for transfers between devices: 12.3 us -> 5.26 us  [weight_grads(): out = both(lax.all_to_all(out, 'z', 0, 0, tiled=True))]
    all_to_all x1, starting transfers between devices: 12.1 us -> 5.83 us  [body(): lax.all_to_all(stage[:, :, :3 * HEAD_DIM].transpose(1, 0, 2, 3), 'z', 0,...]
  transfers between devices with their start and end apart: 6 -> 13, of which waited for: 4 -> 8; matrix products, arithmetic and copies ran while one was open for 11% -> 5% of each run, Pallas kernels for 18% -> 13%
where the time goes in v2:
time: 165 us
  waiting for transfers between devices  51.9 us (31%)
  starting transfers between devices  39.9 us (24%)
  Pallas kernels  23.9 us (14%)
  blocking collectives  15.8 us (10%)
  between operations  15.5 us (9%)
  local copies, waits for them, and re-layouts  10.9 us (7%)
  other arithmetic  4.83 us (3%)
  matrix products  1.78 us (1%)
    all_to_all x1, waiting for transfers between devices, body(): heads = lax.all_to_all(sent, FRAME_AXES, 0, 0, tiled=True)  34.2 us
    pallas_call x1, Pallas kernels, attention(): pl.pallas_call(attn_kernel, out_shape=jax.ShapeDtypeStruct(x.shape, jnp.b...  20 us
    all_to_all x1, blocking collectives, body(): lax.all_to_all(grads.reshape(nx, nz, rows, frames), 'x', 0, 0, tiled=True)  15.8 us
    all_to_all x1, starting transfers between devices, body(): heads = lax.all_to_all(sent, FRAME_AXES, 0, 0, tiled=True)  11.9 us
    ppermute x6, waiting for transfers between devices, shift(): return lax.ppermute(v, axis, [(i, (i + k) % n) for i in range(n)])  10.4 us
    ppermute x6, starting transfers between devices, shift(): return lax.ppermute(v, axis, [(i, (i + k) % n) for i in range(n)])  9.07 us
    ppermute x3, starting transfers between devices, swap_cores(): return lax.ppermute(v, 'core', [(0, 1), (1, 0)])  8.44 us
    unnamed x14, local copies, waits for them, and re-layouts  6 us
  transfers between devices with their start and end apart: 13, of which 8 were waited for; matrix products, arithmetic and copies ran while one was open for 5% of the time, Pallas kernels for 13%

profile of v2, /device:TPU:1, one launch (start us, length us, event | category | flops | bytes accessed | tf_op | source)
XLA Modules:
  0.0 164.6 jit_solution(9882227546112029827)
XLA Ops:
  7.2 0.0 copy-start
  7.2 0.0 all-gather.3.cloned.1.call-start
  7.2 2.0 %pad_maximum_fusion.1 = bf16[2048,128]{1,0:T(8,128)(2,1)} fusion(bf16[1024,128]{1,0:T(8,128)(2,1)} %bitcast.46, bf16[1024,128]{1,0:T(8,128)(2,1)} %bitcast.49), kind=kLoop, calls=%fused_computation.7 | loop fusion | flops 1048576 | bytes 1048576 | tf_op jit(solution)/shard_map/concatenate | solution.py:290
  9.2 0.0 all-gather.3.cloned.1.call-update
  9.3 1.8 %convolution_convert_fusion = bf16[1024,128]{1,0:T(8,128)(2,1)S(1)} fusion(bf16[1024,1024]{1,0:T(8,128)(2,1)S(1)} %copy-done, bf16[1,1024,128]{2,1,0:T(8,128)(2,1)} %param.13), kind=kOutput, calls=%fused_computation | convolution fusion | flops 268566528 | bytes 2621440 | tf_op jit(solution)/shard_map/dot_general | solution.py:291
  11.1 1.1 pad_maximum_fusion
  12.2 11.9 %all-to-all-start = ((bf16[32,128,128]{2,1,0:T(8,128)(2,1)}), bf16[32,128,128]{2,1,0:T(8,128)(2,1)S(1)}, u32[]{:S(2)}, u32[]{:S(2)}) async-start(bf16[32,128,128]{2,1,0:T(8,128)(2,1)} %pad_maximum_fusion), calls=%async_computation | async-start | bytes 2097152 | tf_op jit(solution)/shard_map/all_to_all | solution.py:298
  25.4 0.1 pad_add_fusion.ids_ref
  25.5 34.2 %all-to-all-done.x_ref = bf16[32,128,128]{2,1,0:T(8,128)(2,1)S(1)} async-done(((bf16[32,128,128]{2,1,0:T(8,128)(2,1)}), bf16[32,128,128]{2,1,0:T(8,128)(2,1)S(1)}, u32[]{:S(2)}, u32[]{:S(2)}) %all-to-all-start) | async-done | bytes 1048608 | tf_op jit(solution)/shard_map/all_to_all | solution.py:298
  59.7 20.0 %window_attention.1 = bf16[32,128,128]{2,1,0:T(8,128)(2,1)S(1)} custom-call(s32[3]{0:T(128)S(1)} %pad_add_fusion.ids_ref, bf16[32,128,128]{2,1,0:T(8,128)(2,1)S(1)} %all-to-all-done.x_ref), custom_call_target="tpu_custom_call" | custom-call | flops 2013265920 | bytes 2097152 | tf_op jit(solution)/shard_map/window_attention/pallas_call | solution.py:140
  79.7 15.8 %all_to_all.20.stage_ref = bf16[4,8,128,128]{3,2,1,0:T(8,128)(2,1)S(1)} all-to-all(bf16[4,8,128,128]{3,2,1,0:T(8,128)(2,1)S(1)} %bitcast.44), channel_id=1, replica_groups=mesh['y'=4,'core'=2,'x'=4,'z'=8] {'x'}, dimensions={0} | all-to-all | bytes 2097152 | tf_op jit(solution)/shard_map/all_to_all | solution.py:301
  95.5 2.2 %copy-done.3 = bf16[16384,128]{1,0:T(8,128)(2,1)S(1)} copy-done((bf16[16384,128]{1,0:T(8,128)(2,1)S(1)}, bf16[16384,128]{1,0:T(8,128)(2,1)}, u32[]{:S(2)}) %copy-start.3) | copy-done | bytes 4194328
  97.7 2.1 %weight_grad_terms.1 = bf16[2,4,512,128]{3,2,1,0:T(8,128)(2,1)S(1)} custom-call(s32[3]{0:T(128)S(1)} %pad_add_fusion.ids_ref, bf16[4,8,128,128]{3,2,1,0:T(8,128)(2,1)S(1)} %all_to_all.20.stage_ref, bf16[8,2048,128]{2,1,0:T(8,128)(2,1)S(1)} %bitcast.43), custom_call_target="tpu_custom_call" | custom-call | flops 1073741824 | bytes 6291468 | tf_op jit(solution)/shard_map/weight_grad_terms/pallas_call | solution.py:227
  99.8 1.0 copy-done.2
  100.8 0.8 slice_bitcast_fusion
  101.7 4.1 %collective-permute-start = (bf16[4,512,128]{2,1,0:T(8,128)(2,1)}, bf16[4,512,128]{2,1,0:T(8,128)(2,1)}, u32[]{:S(2)}, u32[]{:S(2)}) collective-permute-start(bf16[4,512,128]{2,1,0:T(8,128)(2,1)} %slice_bitcast_fusion), channel_id=1, source_target_pairs={{0,32},{32,0},{1,33},{33,1},{2,34},{34,2},{3,35},{35,3},{4,36},{36... | collective-permute-start | bytes 1572872 | tf_op jit(solution)/shard_map/ppermute | solution.py:240
  105.7 0.9 copy_bitcast_fusion
  106.7 5.8 %all-to-all-start.2 = ((bf16[8,4,96,128]{3,2,1,0:T(8,128)(2,1)}), bf16[8,4,96,128]{3,2,1,0:T(8,128)(2,1)S(1)}, u32[]{:S(2)}, u32[]{:S(2)}) async-start(bf16[8,4,96,128]{3,2,1,0:T(8,128)(2,1)} %copy_bitcast_fusion), calls=%async_computation.2 | async-start | bytes 1572864 | tf_op jit(solution)/shard_map/all_to_all | solution.py:302
  112.5 1.3 fusion
  113.9 0.6 collective-permute-start.1
  114.5 0.9 collective-permute-start.2
  115.4 1.8 %collective-permute-start.3 = (bf16[512,128]{1,0:T(8,128)(2,1)S(1)}, bf16[512,128]{1,0:T(8,128)(2,1)S(1)}, u32[]{:S(2)}, u32[]{:S(2)}) collective-permute-start(bf16[512,128]{1,0:T(8,128)(2,1)S(1)} %get-tuple-element.8), channel_id=1, source_target_pairs={{0,24},{8,0},{16,8},{24,16},{1,25},{9,1},{17,9},{25,17},{2,26},{10... | collective-permute-start | bytes 393224 | tf_op jit(solution)/shard_map/ppermute | solution.py:245
  117.2 3.1 %collective-permute-done.1 = bf16[512,128]{1,0:T(8,128)(2,1)S(1)} collective-permute-done((bf16[512,128]{1,0:T(8,128)(2,1)S(1)}, bf16[512,128]{1,0:T(8,128)(2,1)S(1)}, u32[]{:S(2)}, u32[]{:S(2)}) %collective-permute-start.1) | collective-permute-done | bytes 131104 | tf_op jit(solution)/shard_map/ppermute | solution.py:245
  120.3 3.4 %collective-permute-done.2 = bf16[512,128]{1,0:T(8,128)(2,1)S(1)} collective-permute-done((bf16[512,128]{1,0:T(8,128)(2,1)S(1)}, bf16[512,128]{1,0:T(8,128)(2,1)S(1)}, u32[]{:S(2)}, u32[]{:S(2)}) %collective-permute-start.2) | collective-permute-done | bytes 131104 | tf_op jit(solution)/shard_map/ppermute | solution.py:245
  123.7 0.1 fusion.2
  123.8 3.1 %collective-permute-start.4 = (bf16[512,128]{1,0:T(8,128)(2,1)S(1)}, bf16[512,128]{1,0:T(8,128)(2,1)S(1)}, u32[]{:S(2)}, u32[]{:S(2)}) collective-permute-start(bf16[512,128]{1,0:T(8,128)(2,1)S(1)} %fusion.2), channel_id=1, source_target_pairs={{0,128},{64,192},{128,0},{192,64},{1,129},{65,193},{129,1},{193,65... | collective-permute-start | bytes 393224 | tf_op jit(solution)/shard_map/ppermute | solution.py:245
  126.9 0.7 collective-permute-start.5
  127.6 2.0 %collective-permute-start.6 = (bf16[512,128]{1,0:T(8,128)(2,1)S(1)}, bf16[512,128]{1,0:T(8,128)(2,1)S(1)}, u32[]{:S(2)}, u32[]{:S(2)}) collective-permute-start(bf16[512,128]{1,0:T(8,128)(2,1)S(1)} %fusion.2), channel_id=1, source_target_pairs={{0,192},{64,0},{128,64},{192,128},{1,193},{65,1},{129,65},{193,129... | collective-permute-start | bytes 393224 | tf_op jit(solution)/shard_map/ppermute | solution.py:245
  129.6 0.5 collective-permute-done.4
  130.0 3.3 %collective-permute-done.5 = bf16[512,128]{1,0:T(8,128)(2,1)S(1)} collective-permute-done((bf16[512,128]{1,0:T(8,128)(2,1)S(1)}, bf16[512,128]{1,0:T(8,128)(2,1)S(1)}, u32[]{:S(2)}, u32[]{:S(2)}) %collective-permute-start.5) | collective-permute-done | bytes 131104 | tf_op jit(solution)/shard_map/ppermute | solution.py:245
  133.4 0.1 collective-permute-done.6
  133.5 0.1 add_convert_fusion
  133.6 0.6 slice.42
  134.2 2.0 %all-to-all-done.2.back_ref = bf16[8,4,96,128]{3,2,1,0:T(8,128)(2,1)S(1)} async-done(((bf16[8,4,96,128]{3,2,1,0:T(8,128)(2,1)}), bf16[8,4,96,128]{3,2,1,0:T(8,128)(2,1)S(1)}, u32[]{:S(2)}, u32[]{:S(2)}) %all-to-all-start.2) | async-done | bytes 786464 | tf_op jit(solution)/shard_map/all_to_all | solution.py:302
  136.2 4.7 %all-to-all-start.3 = ((bf16[8,16,128]{2,1,0:T(8,128)(2,1)}), bf16[8,16,128]{2,1,0:T(8,128)(2,1)S(1)}, u32[]{:S(2)}, u32[]{:S(2)}) async-start(bf16[8,16,128]{2,1,0:T(8,128)(2,1)} %bitcast.16), calls=%async_computation.3 | async-start | bytes 65536 | tf_op jit(solution)/shard_map/all_to_all | solution.py:273
  140.8 1.7 %collective-permute-start.7 = (bf16[384,128]{1,0:T(8,128)(2,1)S(1)}, bf16[384,128]{1,0:T(8,128)(2,1)S(1)}, u32[]{:S(2)}, u32[]{:S(2)}) collective-permute-start(bf16[384,128]{1,0:T(8,128)(2,1)S(1)} %slice.44), channel_id=1, source_target_pairs={{0,32},{32,0},{1,33},{33,1},{2,34},{34,2},{3,35},{35,3},{4,36},{36... | collective-permute-start | bytes 294920 | tf_op jit(solution)/shard_map/ppermute | solution.py:240
  142.5 5.3 %all-to-all-done.3 = bf16[8,16,128]{2,1,0:T(8,128)(2,1)S(1)} async-done(((bf16[8,16,128]{2,1,0:T(8,128)(2,1)}), bf16[8,16,128]{2,1,0:T(8,128)(2,1)S(1)}, u32[]{:S(2)}, u32[]{:S(2)}) %all-to-all-start.3) | async-done | bytes 32800 | tf_op jit(solution)/shard_map/all_to_all | solution.py:273
  147.8 2.7 %collective-permute-start.8 = (bf16[8,16,128]{2,1,0:T(8,128)(2,1)S(1)}, bf16[8,16,128]{2,1,0:T(8,128)(2,1)S(1)}, u32[]{:S(2)}, u32[]{:S(2)}) collective-permute-start(bf16[8,16,128]{2,1,0:T(8,128)(2,1)S(1)} %all-to-all-done.3), channel_id=1, source_target_pairs={{0,32},{32,0},{1,33},{33,1},{2,34},{34,2},{3,35},{35,3},{4,36},{36... | collective-permute-start | bytes 98312 | tf_op jit(solution)/shard_map/ppermute | solution.py:240
  150.5 2.8 %copy-done.1 = bf16[1024,3072]{1,0:T(8,128)(2,1)S(1)} copy-done((bf16[1024,3072]{1,0:T(8,128)(2,1)S(1)}, bf16[1024,3072]{1,0:T(8,128)(2,1)}, u32[]{:S(2)}) %copy-start.1) | copy-done | bytes 6291480
  153.2 1.8 %input_grad.1 = bf16[1024,128]{1,0:T(8,128)(2,1)} custom-call(bf16[1024,3072]{1,0:T(8,128)(2,1)S(1)} %copy-done.1, bf16[8,4,96,128]{3,2,1,0:T(8,128)(2,1)S(1)} %all-to-all-done.2.back_ref), custom_call_target="tpu_custom_call" | custom-call | flops 805306368 | bytes 7340032 | tf_op jit(solution)/shard_map/input_grad/pallas_call | solution.py:227
  155.1 0.1 stack.45
  155.2 0.1 copy.27
  155.3 0.1 stack.46
  155.4 0.1 copy.28
  155.5 0.1 convert_bitcast_fusion
  155.6 0.9 reshape.55
  156.6 0.3 copy.26
  156.8 0.9 reshape.54
  (18 shorter events, 0.1 us)
Async XLA Ops:
  7.2 2.1 %copy-start = (bf16[1024,1024]{1,0:T(8,128)(2,1)S(1)}, bf16[1024,1024]{1,0:T(8,128)(2,1)}, u32[]{:S(2)}) copy-start(bf16[1024,1024]{1,0:T(8,128)(2,1)} %param.15) | copy-start | bytes 6291460
  7.2 88.3 %all-gather.3.cloned.1.call-start = ((), (), s32[]{:S(2)}) async-start(), calls=%async_computation.4 | async-start | bytes 4718592 | tf_op jit(solution)/shard_map/all_gather | solution.py:290
  9.3 1.8 %copy-start.4 = (bf16[1,1024,128]{2,1,0:T(8,128)(2,1)S(1)}, bf16[1,1024,128]{2,1,0:T(8,128)(2,1)}, u32[]{:S(2)}) copy-start(bf16[1,1024,128]{2,1,0:T(8,128)(2,1)} %param.12) | copy-start | bytes 786436
  9.3 1.8 %copy-start.5 = (bf16[1,1024,128]{2,1,0:T(8,128)(2,1)S(1)}, bf16[1,1024,128]{2,1,0:T(8,128)(2,1)}, u32[]{:S(2)}) copy-start(bf16[1,1024,128]{2,1,0:T(8,128)(2,1)} %param.11) | copy-start | bytes 786436
  9.3 1.8 %copy-start.6 = (bf16[1,1024,128]{2,1,0:T(8,128)(2,1)S(1)}, bf16[1,1024,128]{2,1,0:T(8,128)(2,1)}, u32[]{:S(2)}) copy-start(bf16[1,1024,128]{2,1,0:T(8,128)(2,1)} %param.10) | copy-start | bytes 786436
  12.2 47.5 %all-to-all-start = ((bf16[32,128,128]{2,1,0:T(8,128)(2,1)}), bf16[32,128,128]{2,1,0:T(8,128)(2,1)S(1)}, u32[]{:S(2)}, u32[]{:S(2)}) async-start(bf16[32,128,128]{2,1,0:T(8,128)(2,1)} %pad_maximum_fusion), calls=%async_computation | async-start | bytes 2097152 | tf_op jit(solution)/shard_map/all_to_all | solution.py:298
  95.5 2.2 %copy-start.3 = (bf16[16384,128]{1,0:T(8,128)(2,1)S(1)}, bf16[16384,128]{1,0:T(8,128)(2,1)}, u32[]{:S(2)}) copy-start(bf16[16384,128]{1,0:T(8,128)(2,1)} %all-gather.3.cloned.1.call-done) | copy-start | bytes 12582916
  99.8 1.0 copy-start.2
  101.7 10.8 %collective-permute-start = (bf16[4,512,128]{2,1,0:T(8,128)(2,1)}, bf16[4,512,128]{2,1,0:T(8,128)(2,1)}, u32[]{:S(2)}, u32[]{:S(2)}) collective-permute-start(bf16[4,512,128]{2,1,0:T(8,128)(2,1)} %slice_bitcast_fusion), channel_id=1, source_target_pairs={{0,32},{32,0},{1,33},{33,1},{2,34},{34,2},{3,35},{35,3},{4,36},{36... | collective-permute-start | bytes 1572872 | tf_op jit(solution)/shard_map/ppermute | solution.py:240
  106.7 29.5 %all-to-all-start.2 = ((bf16[8,4,96,128]{3,2,1,0:T(8,128)(2,1)}), bf16[8,4,96,128]{3,2,1,0:T(8,128)(2,1)S(1)}, u32[]{:S(2)}, u32[]{:S(2)}) async-start(bf16[8,4,96,128]{3,2,1,0:T(8,128)(2,1)} %copy_bitcast_fusion), calls=%async_computation.2 | async-start | bytes 1572864 | tf_op jit(solution)/shard_map/all_to_all | solution.py:302
  113.9 6.4 %collective-permute-start.1 = (bf16[512,128]{1,0:T(8,128)(2,1)S(1)}, bf16[512,128]{1,0:T(8,128)(2,1)S(1)}, u32[]{:S(2)}, u32[]{:S(2)}) collective-permute-start(bf16[512,128]{1,0:T(8,128)(2,1)S(1)} %get-tuple-element.7), channel_id=1, source_target_pairs={{0,16},{8,24},{16,0},{24,8},{1,17},{9,25},{17,1},{25,9},{2,18},{10... | collective-permute-start | bytes 393224 | tf_op jit(solution)/shard_map/ppermute | solution.py:245
  114.5 9.2 %collective-permute-start.2 = (bf16[512,128]{1,0:T(8,128)(2,1)S(1)}, bf16[512,128]{1,0:T(8,128)(2,1)S(1)}, u32[]{:S(2)}, u32[]{:S(2)}) collective-permute-start(bf16[512,128]{1,0:T(8,128)(2,1)S(1)} %get-tuple-element.9), channel_id=1, source_target_pairs={{0,8},{8,16},{16,24},{24,0},{1,9},{9,17},{17,25},{25,1},{2,10},{10... | collective-permute-start | bytes 393224 | tf_op jit(solution)/shard_map/ppermute | solution.py:245
  115.4 8.3 %collective-permute-start.3 = (bf16[512,128]{1,0:T(8,128)(2,1)S(1)}, bf16[512,128]{1,0:T(8,128)(2,1)S(1)}, u32[]{:S(2)}, u32[]{:S(2)}) collective-permute-start(bf16[512,128]{1,0:T(8,128)(2,1)S(1)} %get-tuple-element.8), channel_id=1, source_target_pairs={{0,24},{8,0},{16,8},{24,16},{1,25},{9,1},{17,9},{25,17},{2,26},{10... | collective-permute-start | bytes 393224 | tf_op jit(solution)/shard_map/ppermute | solution.py:245
  123.8 6.3 %collective-permute-start.4 = (bf16[512,128]{1,0:T(8,128)(2,1)S(1)}, bf16[512,128]{1,0:T(8,128)(2,1)S(1)}, u32[]{:S(2)}, u32[]{:S(2)}) collective-permute-start(bf16[512,128]{1,0:T(8,128)(2,1)S(1)} %fusion.2), channel_id=1, source_target_pairs={{0,128},{64,192},{128,0},{192,64},{1,129},{65,193},{129,1},{193,65... | collective-permute-start | bytes 393224 | tf_op jit(solution)/shard_map/ppermute | solution.py:245
  126.9 6.5 %collective-permute-start.5 = (bf16[512,128]{1,0:T(8,128)(2,1)S(1)}, bf16[512,128]{1,0:T(8,128)(2,1)S(1)}, u32[]{:S(2)}, u32[]{:S(2)}) collective-permute-start(bf16[512,128]{1,0:T(8,128)(2,1)S(1)} %fusion.2), channel_id=1, source_target_pairs={{0,64},{64,128},{128,192},{192,0},{1,65},{65,129},{129,193},{193,1... | collective-permute-start | bytes 393224 | tf_op jit(solution)/shard_map/ppermute | solution.py:245
  127.6 5.9 %collective-permute-start.6 = (bf16[512,128]{1,0:T(8,128)(2,1)S(1)}, bf16[512,128]{1,0:T(8,128)(2,1)S(1)}, u32[]{:S(2)}, u32[]{:S(2)}) collective-permute-start(bf16[512,128]{1,0:T(8,128)(2,1)S(1)} %fusion.2), channel_id=1, source_target_pairs={{0,192},{64,0},{128,64},{192,128},{1,193},{65,1},{129,65},{193,129... | collective-permute-start | bytes 393224 | tf_op jit(solution)/shard_map/ppermute | solution.py:245
  136.2 11.6 %all-to-all-start.3 = ((bf16[8,16,128]{2,1,0:T(8,128)(2,1)}), bf16[8,16,128]{2,1,0:T(8,128)(2,1)S(1)}, u32[]{:S(2)}, u32[]{:S(2)}) async-start(bf16[8,16,128]{2,1,0:T(8,128)(2,1)} %bitcast.16), calls=%async_computation.3 | async-start | bytes 65536 | tf_op jit(solution)/shard_map/all_to_all | solution.py:273
  140.8 15.7 %collective-permute-start.7 = (bf16[384,128]{1,0:T(8,128)(2,1)S(1)}, bf16[384,128]{1,0:T(8,128)(2,1)S(1)}, u32[]{:S(2)}, u32[]{:S(2)}) collective-permute-start(bf16[384,128]{1,0:T(8,128)(2,1)S(1)} %slice.44), channel_id=1, source_target_pairs={{0,32},{32,0},{1,33},{33,1},{2,34},{34,2},{3,35},{35,3},{4,36},{36... | collective-permute-start | bytes 294920 | tf_op jit(solution)/shard_map/ppermute | solution.py:240
  147.8 7.5 %collective-permute-start.8 = (bf16[8,16,128]{2,1,0:T(8,128)(2,1)S(1)}, bf16[8,16,128]{2,1,0:T(8,128)(2,1)S(1)}, u32[]{:S(2)}, u32[]{:S(2)}) collective-permute-start(bf16[8,16,128]{2,1,0:T(8,128)(2,1)S(1)} %all-to-all-done.3), channel_id=1, source_target_pairs={{0,32},{32,0},{1,33},{33,1},{2,34},{34,2},{3,35},{35,3},{4,36},{36... | collective-permute-start | bytes 98312 | tf_op jit(solution)/shard_map/ppermute | solution.py:240
  150.5 2.8 %copy-start.1 = (bf16[1024,3072]{1,0:T(8,128)(2,1)S(1)}, bf16[1024,3072]{1,0:T(8,128)(2,1)}, u32[]{:S(2)}) copy-start(bf16[1024,3072]{1,0:T(8,128)(2,1)} %w_ref.1) | copy-start | bytes 18874372
Sparse Core Ops, SparseCore 0:
  9.8 80.4 all-gather.2

commit v3 on v2

v3 whole, which is shorter than its diff:
```python
import math

import jax
import jax.numpy as jnp
from jax import lax
from jax.experimental import pallas as pl
from jax.experimental.pallas import tpu as pltpu
from jax.sharding import Mesh, PartitionSpec as P

HEAD_DIM = 32
HALF = 512
QT = 256
BLK = 128
GROUP = 4
UNROLL = 16
masked_score = -1e30
REC_AXES = ("y", "core")
FRAME_AXES = ("x", "z")
NT = (((1,), (1,)), ((), ()))


def attn_kernel(ids_ref, x_ref, *refs):
    parts, (gq_ref, ao_ref, kv_t, k_p, v_p, acc) = refs[:-6], refs[-6:]
    nx, nz = len(parts), parts[0].shape[0]
    own_x = ids_ref[1]
    blocks = x_ref.shape[0]
    seq = blocks * BLK
    span = QT + 2 * HALF
    scale = 1.0 / math.sqrt(HEAD_DIM)
    live = ids_ref[0]
    f32, bf = jnp.float32, jnp.bfloat16

    zpad = jnp.zeros((HALF, BLK), bf)
    dead = jnp.where(lax.broadcasted_iota(jnp.int32, (HALF, BLK), 1) == HEAD_DIM, masked_score, 0.0).astype(bf)
    kv_t[0:HALF, :] = dead
    kv_t[HALF + seq :, :] = dead
    zl = jnp.zeros((HEAD_DIM, HALF), bf)
    for ref in (k_p, v_p):
        ref[:, 0:HALF] = zl
        ref[:, HALF + seq :] = zl
    acc[...] = jnp.zeros_like(acc)
    row_frame = lax.broadcasted_iota(jnp.int32, (HEAD_DIM, BLK), 1)
    row_id = lax.broadcasted_iota(jnp.int32, (HEAD_DIM, BLK), 0)

    def prep(b, _):
        start = pl.multiple_of(HALF + b * BLK, BLK)
        k_blk = x_ref[b, HEAD_DIM : 2 * HEAD_DIM, :]
        v_blk = x_ref[b, 2 * HEAD_DIM : 3 * HEAD_DIM, :]
        k_p[:, pl.ds(start, BLK)] = k_blk
        v_p[:, pl.ds(start, BLK)] = v_blk
        bias = jnp.where((row_id == 0) & (row_frame + b * BLK >= live), masked_score, 0.0)
        wide = jnp.concatenate(
            [k_blk.astype(f32), bias, v_blk.astype(f32), jnp.zeros((HEAD_DIM, BLK), f32)], axis=0
        )
        kv_t[pl.ds(start, BLK), :] = wide.T.astype(bf)
        return 0

    lax.fori_loop(0, blocks, prep, 0, unroll=UNROLL)

    b_id = lax.broadcasted_iota(jnp.int32, (QT, QT), 0)
    a_id = lax.broadcasted_iota(jnp.int32, (QT, QT), 1)
    ones_row = jnp.where(lax.broadcasted_iota(jnp.int32, (HEAD_DIM, QT), 0) == 0, 1.0, 0.0).astype(bf)
    z64 = jnp.zeros((2 * HEAD_DIM, QT), bf)
    z32 = jnp.zeros((HEAD_DIM, QT), bf)
    c = scale * math.log2(math.e)

    def dot(a, b):
        return jnp.dot(a, b, preferred_element_type=f32)

    below = b_id > a_id
    above = b_id < a_id

    def group(n, _):
        tiles = [n * GROUP + j for j in range(GROUP)]
        bases = [pl.multiple_of(i * QT, QT) for i in tiles]
        qs, gs = [], []
        for i in tiles:
            x0, x1 = x_ref[2 * i], x_ref[2 * i + 1]
            q = jnp.concatenate([x0[0:32], x1[0:32]], axis=1)
            g = jnp.concatenate([x0[96:128], x1[96:128]], axis=1)
            qs.append(jnp.concatenate([q, ones_row, z64], axis=0))
            gs.append(jnp.concatenate([z64, g, z32], axis=0))
        kvs = [kv_t[pl.ds(b, span), :] for b in bases]
        ss = [dot(kv, r) for kv, r in zip(kvs, qs)]
        pgs = [dot(kv, r) for kv, r in zip(kvs, gs)]
        mids, edges, ps, aos = [], [], [], []
        for j in range(GROUP):
            s = ss[j]
            edge = jnp.where(below, s[0:QT], jnp.where(above, s[span - QT :], masked_score))
            mid = s[QT : span - QT]
            m = jnp.maximum(jnp.max(mid, axis=0, keepdims=True), jnp.max(edge, axis=0, keepdims=True))
            mid = jnp.exp2((mid - m) * c)
            edge = jnp.exp2((edge - m) * c)
            total = jnp.sum(mid, axis=0, keepdims=True) + jnp.sum(edge, axis=0, keepdims=True)
            q_live = bases[j] + lax.broadcasted_iota(jnp.int32, (1, QT), 1) < live
            inv = jnp.where(q_live, 1.0 / total, 0.0)
            mid = mid * inv
            edge = edge * inv
            p = jnp.concatenate(
                [jnp.where(below, edge, 0.0).astype(bf), mid.astype(bf), jnp.where(above, edge, 0.0).astype(bf)],
                axis=0,
            )
            mids.append(mid)
            edges.append(edge)
            ps.append(p)
            aos.append(dot(v_p[:, pl.ds(bases[j], span)], p).astype(bf))
        dss, gqs = [], []
        for j in range(GROUP):
            pg = pgs[j]
            rd = jnp.sum(gs[j][64:96].astype(f32) * aos[j].astype(f32), axis=0, keepdims=True)
            d_mid = mids[j] * (pg[QT : span - QT] - rd)
            d_edge = edges[j] * (jnp.where(below, pg[0:QT], pg[span - QT :]) - rd)
            ds = jnp.concatenate(
                [jnp.where(below, d_edge, 0.0).astype(bf), d_mid.astype(bf), jnp.where(above, d_edge, 0.0).astype(bf)],
                axis=0,
            )
            dss.append(ds)
            gqs.append((dot(k_p[:, pl.ds(bases[j], span)], ds) * scale).astype(bf))
        for j in range(GROUP):
            acc[pl.ds(bases[j], span), :] += dot(dss[j], qs[j].T) + dot(ps[j], gs[j].T)
        for j in range(GROUP):
            for half in range(2):
                sl = slice(half * BLK, (half + 1) * BLK)
                gq_ref[2 * tiles[j] + half] = gqs[j][:, sl]
                ao_ref[2 * tiles[j] + half] = aos[j][:, sl]
        return 0

    lax.fori_loop(0, seq // QT // GROUP, group, 0)

    for k in range(nx):
        for z in range(nz):
            b = lax.rem(own_x + k, nx) * nz + z
            start = pl.multiple_of(HALF + b * BLK, BLK)
            t = acc[pl.ds(start, BLK), :].T
            gk = (t[0:HEAD_DIM] * scale).astype(bf)
            gv = t[2 * HEAD_DIM : 3 * HEAD_DIM].astype(bf)
            parts[k][z] = jnp.concatenate([gq_ref[b], gk, gv, ao_ref[b]], axis=0)


def attention(x, ids, nx, nz):
    blocks = x.shape[0]
    seq = blocks * BLK
    padded = seq + 2 * HALF
    return kernel_call(
        attn_kernel,
        "window_attention",
        [pltpu.SMEM, pltpu.VMEM],
        [(nz, 4 * HEAD_DIM, BLK)] * nx,
        [
            pltpu.VMEM((blocks, HEAD_DIM, BLK), jnp.bfloat16),
            pltpu.VMEM((blocks, HEAD_DIM, BLK), jnp.bfloat16),
            pltpu.VMEM((padded, BLK), jnp.bfloat16),
            pltpu.VMEM((HEAD_DIM, padded), jnp.bfloat16),
            pltpu.VMEM((HEAD_DIM, padded), jnp.bfloat16),
            pltpu.VMEM((padded, BLK), jnp.float32),
        ],
        6 * 2 * seq * (QT + 2 * HALF) * HEAD_DIM,
        ids,
        x,
        exps=seq * 2 * HALF,
    )


def kernel_call(kernel, name, spaces, out_shapes, scratch, flops, *args, exps=0):
    outs = [jax.ShapeDtypeStruct(shape, jnp.bfloat16) for shape in out_shapes]
    return pl.pallas_call(
        kernel,
        out_shape=outs,
        in_specs=[pl.BlockSpec(memory_space=space) for space in spaces],
        out_specs=[pl.BlockSpec(memory_space=pltpu.VMEM)] * len(outs),
        scratch_shapes=scratch,
        compiler_params=pltpu.CompilerParams(vmem_limit_bytes=40 << 20),
        cost_estimate=pl.CostEstimate(
            flops=flops,
            bytes_accessed=sum(a.size * a.dtype.itemsize for a in args)
            + 2 * sum(math.prod(s) for s in out_shapes),
            transcendentals=exps,
        ),
        name=name,
    )(*args)


def terms_kernel(ids_ref, *refs):
    parts, (gathered_ref, mine_ref, other_ref, ao_ref) = refs[:-4], refs[-4:]
    own_x, own_core = ids_ref[1], ids_ref[2]
    nx = len(parts)
    nz, rows, frames = parts[0].shape
    width = gathered_ref.shape[1] // 2
    g_rows = 3 * HEAD_DIM
    f32, bf = jnp.float32, jnp.bfloat16
    chunk = 2 * BLK
    half = width // 2

    def wide(part):
        return [jnp.concatenate([part(k), part(k + 1)], axis=1) for k in range(0, nz, 2)]

    def gathered(start):
        return wide(lambda k: gathered_ref[k, pl.ds(start, chunk), :])

    def product(lefts, rights):
        return sum(
            lax.dot_general(a, b, NT, preferred_element_type=f32) for a, b in zip(lefts, rights)
        )

    for k in range(nx):
        ao_ref[lax.rem(own_x - k + nx, nx)] = parts[k][:, g_rows:, :]
    grads = wide(lambda z: jnp.concatenate([part[z, :g_rows, :] for part in parts], axis=0))
    aos = wide(lambda z: ao_ref[:, z].reshape(nx * HEAD_DIM, frames))
    chunks = half // chunk
    for slot, out_ref in ((1, other_ref), (0, mine_ref)):
        for n in range(chunks):
            start = pl.multiple_of(lax.rem(own_core + slot, 2) * half + n * chunk, chunk)
            total = product(grads, gathered(start)).astype(bf).reshape(nx, g_rows, chunk)
            for k in range(nx):
                for j in range(2):
                    b = n * 2 + j
                    out_ref[(nx - k) % nx, b * g_rows : (b + 1) * g_rows, :] = total[
                        k, :, j * BLK : (j + 1) * BLK
                    ]
    sub = HEAD_DIM // 2
    first = 2 * chunks * g_rows
    for x in range(nx):
        to = lax.rem(x - own_x + nx, nx)
        total = product(gathered(width + x * chunk), aos).reshape(nz, 2, sub, nx * HEAD_DIM)
        low, high = (total[:, core].reshape(nz * sub, nx * HEAD_DIM) for core in range(2))
        mine_ref[to, first:, :] = jnp.where(own_core == 0, low, high).astype(bf)
        other_ref[to, first:, :] = jnp.where(own_core == 0, high, low).astype(bf)


def weight_terms(ids, parts, gathered):
    nx = len(parts)
    nz, rows, frames = parts[0].shape
    width = gathered.shape[1] // 2
    out = (nx, width // 2 // BLK * 3 * HEAD_DIM + nz * HEAD_DIM // 2, BLK)
    return kernel_call(
        terms_kernel,
        "weight_grad_terms",
        [pltpu.SMEM] + [pltpu.VMEM] * (nx + 1),
        [out, out],
        [pltpu.VMEM((nx, nz, HEAD_DIM, frames), jnp.bfloat16)],
        2 * nx * rows * width * nz * frames,
        ids,
        *parts,
        gathered,
    )


def own_weights_kernel(ids_ref, w_ref, out_ref, buf, sems):
    own_x, own_z = ids_ref[1], ids_ref[3]
    nx, rows, cols = buf.shape
    width = out_ref.shape[0]
    nz = w_ref.shape[0] // rows // nx
    copies = []
    for k in range(nx):
        head = lax.rem(own_x - k + nx, nx) * nz + own_z
        start = pl.multiple_of(head * rows, rows)
        copies.append(
            pltpu.make_async_copy(w_ref.at[pl.ds(start, rows), :], buf.at[k], sems.at[k])
        )
    for copy in copies:
        copy.start()
    for copy in copies:
        copy.wait()
    own = jnp.concatenate(
        [buf[k, :, i * width : (i + 1) * width] for k in range(nx) for i in range(cols // width)],
        axis=0,
    )
    out_ref[...] = own.T


def own_weights(ids, w_qkv, nx):
    width, cols = w_qkv.shape
    return kernel_call(
        own_weights_kernel,
        "own_weights",
        [pltpu.SMEM, pl.ANY],
        [(width, nx * 3 * HEAD_DIM)],
        [pltpu.VMEM((nx, HEAD_DIM, cols), jnp.bfloat16), pltpu.SemaphoreType.DMA((nx,))],
        0,
        ids,
        w_qkv,
    )[0]


def input_terms_kernel(weights_ref, *refs):
    parts, out_ref = refs[:-1], refs[-1]
    g_rows = 3 * HEAD_DIM
    for z in range(0, out_ref.shape[0], 2):
        grads = jnp.concatenate(
            [
                jnp.concatenate([part[z + j, :g_rows, :] for part in parts], axis=0)
                for j in range(2)
            ],
            axis=1,
        )
        total = jnp.dot(weights_ref[...], grads, preferred_element_type=jnp.float32)
        total = total.astype(jnp.bfloat16)
        for j in range(2):
            out_ref[z + j] = total[:, j * BLK : (j + 1) * BLK]


def input_terms(weights, parts):
    width, rows = weights.shape
    nz = parts[0].shape[0]
    return kernel_call(
        input_terms_kernel,
        "input_terms",
        [pltpu.VMEM] * (1 + len(parts)),
        [(nz, width, BLK)],
        [],
        2 * width * rows * nz * BLK,
        weights,
        *parts,
    )[0]


def swap_cores(v):
    return lax.ppermute(v, "core", [(0, 1), (1, 0)])


def shift(v, axis, k):
    n = lax.axis_size(axis)
    return lax.ppermute(v, axis, [(i, (i + k) % n) for i in range(n)])


def add_up(*terms):
    terms = [t.astype(jnp.float32) for t in terms]
    while len(terms) > 1:
        terms = [a + b for a, b in zip(terms[::2], terms[1::2])]
    return terms[0].astype(jnp.bfloat16)


def sum_over_y(v):
    v = add_up(v, lax.ppermute(v, "y", [(0, 1), (1, 0), (2, 3), (3, 2)]))
    return add_up(v, lax.ppermute(v, "y", [(0, 3), (3, 0), (1, 2), (2, 1)]))


def weight_grads(mine, other, width):
    nz = lax.axis_size("z")
    core = lax.axis_index("core")
    mine = add_up(mine, swap_cores(other))
    mine = add_up(mine[0], shift(mine[2], "x", 2), shift(mine[1], "x", 1), shift(mine[3], "x", 3))
    rows = width // 2 // BLK * 3 * HEAD_DIM
    mine = sum_over_y(mine)

    def both(part):
        other = swap_cores(part)
        return jnp.where(core == 0, jnp.stack([part, other]), jnp.stack([other, part]))

    out = mine[rows:].reshape(nz, HEAD_DIM // 2, BLK)
    out = lax.all_to_all(out, "z", 0, 0, tiled=True)
    qkv = both(mine[:rows]).reshape(2, -1, 3, HEAD_DIM, BLK)
    dw_qkv = qkv.transpose(3, 2, 0, 1, 4).reshape(HEAD_DIM, 3 * width).astype(jnp.float32)
    out, dw_qkv = lax.optimization_barrier((out, dw_qkv))
    out = both(out).reshape(2, nz, HEAD_DIM // 2, BLK // HEAD_DIM, HEAD_DIM)
    dw_out = out.transpose(0, 2, 3, 1, 4).reshape(HEAD_DIM, width).astype(jnp.float32)
    return dw_qkv, dw_out


def body(normed, query_act, key_act, value_act, grad_out, w_qkv, w_out, lengths, offsets):
    f32, bf = jnp.float32, jnp.bfloat16
    nx, nz = lax.axis_size("x"), lax.axis_size("z")
    shards = nx * nz
    width = w_out.shape[0]
    frames = normed.shape[2]
    seq_len = frames * shards
    live = jnp.clip(lengths[0] - offsets[0], 0, seq_len)
    ids = jnp.stack([live] + [lax.axis_index(a) for a in ("x", "core", "z")]).astype(jnp.int32)
    own_grad = grad_out[0]
    head_grad = lax.dot_general(
        w_out, own_grad, (((0,), (0,)), ((), ())), preferred_element_type=f32
    ).astype(bf)
    sent = jnp.concatenate(
        [a.reshape(shards, HEAD_DIM, frames) for a in (query_act[0], key_act[0], value_act[0], head_grad)],
        axis=1,
    )
    heads = lax.all_to_all(sent, FRAME_AXES, 0, 0, tiled=True)
    own, _ = lax.optimization_barrier(((normed[0], own_grad), sent))
    gathered = lax.all_gather(jnp.concatenate(own, axis=0), "z")
    weights = own_weights(ids, w_qkv, nx)
    heads, weights = lax.optimization_barrier((heads, weights))
    parts = attention(heads, ids, nx, nz)
    parts = [parts[0]] + [shift(parts[k], "x", k) for k in range(1, nx)]
    terms = input_terms(weights, parts).reshape(nz * width, frames)
    grad_normed = lax.psum_scatter(terms, "z", scatter_dimension=0, tiled=True)
    mine, other = weight_terms(ids, parts, gathered)
    dw_qkv, dw_out = weight_grads(mine, other, width)
    return (grad_normed[None], dw_qkv, dw_out)


def solution(mesh):
    chips = Mesh(mesh.devices.reshape(4, 2, 4, 8), ("y", "core", "x", "z"))
    data = P(REC_AXES, None, FRAME_AXES)
    return jax.shard_map(
        body,
        mesh=chips,
        in_specs=(data, data, data, data, data, P(), P(), P(REC_AXES), P(REC_AXES)),
        out_specs=(data, P(FRAME_AXES, None), P(FRAME_AXES, None)),
        check_vma=False,
    )
```

time: 165 us -> 154 us (0.933)
  blocking collectives: 15.8 us -> 0 us
  starting transfers between devices: 39.9 us -> 44.5 us
  other arithmetic: 4.83 us -> 2.52 us
  Pallas kernels: 23.9 us -> 25.8 us
    all_to_all x1 -> x0, blocking collectives: 15.8 us -> none  [body(): lax.all_to_all(grads.reshape(nx, nz, rows, frames), 'x', 0, 0, tiled=True)]
    all_to_all x1, waiting for transfers between devices: 34.2 us -> 25 us  [body(): heads = lax.all_to_all(sent, FRAME_AXES, 0, 0, tiled=True)]
    ppermute x0 -> x2, waiting for transfers between devices: none -> 5.69 us  [the longest x1 2.98 us: sum_over_y(): v = add_up(v, lax.ppermute(v, 'y', [(0, 1), (1, 0), (2, 3), (3, 2)]))]
    ppermute x0 -> x2, starting transfers between devices: none -> 4.38 us  [the longest x1 3.05 us: sum_over_y(): return add_up(v, lax.ppermute(v, 'y', [(0, 3), (3, 0), (1, 2), (2, 1)]))]
    ppermute x6, waiting for transfers between devices: 10.4 us -> 13.1 us  [shift(): return lax.ppermute(v, axis, [(i, (i + k) % n) for i in range(n)])]
    ppermute x3, starting transfers between devices: 8.44 us -> 11.1 us  [swap_cores(): return lax.ppermute(v, 'core', [(0, 1), (1, 0)])]
    all_to_all x2 -> x1, starting transfers between devices: 10.5 us -> 8 us  [weight_grads(): out = lax.all_to_all(out, 'z', 0, 0, tiled=True)]
    ppermute x3, waiting for transfers between devices: 0.01 us -> 2.19 us  [swap_cores(): return lax.ppermute(v, 'core', [(0, 1), (1, 0)])]
  transfers between devices with their start and end apart: 13 -> 15, of which waited for: 8 -> 11; matrix products, arithmetic and copies ran while one was open for 5% -> 2% of each run, Pallas kernels for 13% -> 17%
where the time goes in v3:
time: 154 us
  waiting for transfers between devices  52.5 us (34%)
  starting transfers between devices  44.5 us (29%)
  Pallas kernels  25.8 us (17%)
  between operations  15.6 us (10%)
  local copies, waits for them, and re-layouts  11.2 us (7%)
  other arithmetic  2.52 us (2%)
  matrix products  1.71 us (1%)
    pallas_call x4, Pallas kernels, kernel_call(): pl.pallas_call(kernel, out_shape=outs, in_specs=[pl.BlockSpec(memory_spac...  25.8 us
    all_to_all x1, waiting for transfers between devices, body(): heads = lax.all_to_all(sent, FRAME_AXES, 0, 0, tiled=True)  25 us
    ppermute x6, waiting for transfers between devices, shift(): return lax.ppermute(v, axis, [(i, (i + k) % n) for i in range(n)])  13.1 us
    all_to_all x1, starting transfers between devices, body(): heads = lax.all_to_all(sent, FRAME_AXES, 0, 0, tiled=True)  12 us
    ppermute x3, starting transfers between devices, swap_cores(): return lax.ppermute(v, 'core', [(0, 1), (1, 0)])  11.1 us
    ppermute x6, starting transfers between devices, shift(): return lax.ppermute(v, axis, [(i, (i + k) % n) for i in range(n)])  8.97 us
    unnamed x26, local copies, waits for them, and re-layouts  8.12 us
    all_to_all x1, starting transfers between devices, weight_grads(): out = lax.all_to_all(out, 'z', 0, 0, tiled=True)  8 us
  transfers between devices with their start and end apart: 15, of which 11 were waited for; matrix products, arithmetic and copies ran while one was open for 2% of the time, Pallas kernels for 17%

profile of v3, /device:TPU:1, one launch (start us, length us, event | category | flops | bytes accessed | tf_op | source)
XLA Modules:
  0.0 153.9 jit_solution(10708645717429888431)
XLA Ops:
  7.3 1.5 copy-done
  8.8 1.7 %convolution_convert_fusion = bf16[1024,128]{1,0:T(8,128)(2,1)S(1)} fusion(bf16[1024,1024]{1,0:T(8,128)(2,1)S(1)} %copy-done, bf16[1,1024,128]{2,1,0:T(8,128)(2,1)} %param.13), kind=kOutput, calls=%fused_computation | convolution fusion | flops 268566528 | bytes 2621440 | tf_op jit(solution)/shard_map/dot_general | solution.py:370
  10.5 1.2 pad_maximum_fusion
  11.7 0.8 pad_maximum_fusion.1
  12.6 12.0 %all-to-all-start = ((bf16[32,128,128]{2,1,0:T(8,128)(2,1)}), bf16[32,128,128]{2,1,0:T(8,128)(2,1)}, u32[]{:S(2)}, u32[]{:S(2)}) async-start(bf16[32,128,128]{2,1,0:T(8,128)(2,1)} %pad_maximum_fusion), calls=%async_computation | async-start | bytes 2097152 | tf_op jit(solution)/shard_map/all_to_all | solution.py:377
  24.6 0.0 reduce-scatter.2.cloned.1.call-start
  25.9 0.1 pad_add_fusion.ids_ref
  26.0 3.0 %copy-done.2 = bf16[1024,3072]{1,0:T(8,128)(2,1)S(1)} copy-done((bf16[1024,3072]{1,0:T(8,128)(2,1)S(1)}, bf16[1024,3072]{1,0:T(8,128)(2,1)}, u32[]{:S(2)}) %copy-start.2) | copy-done | bytes 6291480
  29.0 1.9 %own_weights.1.weights_ref = bf16[1024,384]{1,0:T(8,128)(2,1)S(1)} custom-call(s32[4]{0:T(128)S(1)} %pad_add_fusion.ids_ref, bf16[1024,3072]{1,0:T(8,128)(2,1)S(1)} %copy-done.2), custom_call_target="tpu_custom_call" | custom-call | bytes 7077904 | tf_op jit(solution)/shard_map/own_weights/pallas_call | solution.py:166
  30.9 25.0 %all-to-all-done.x_ref = bf16[32,128,128]{2,1,0:T(8,128)(2,1)} async-done(((bf16[32,128,128]{2,1,0:T(8,128)(2,1)}), bf16[32,128,128]{2,1,0:T(8,128)(2,1)}, u32[]{:S(2)}, u32[]{:S(2)}) %all-to-all-start) | async-done | bytes 1048608 | tf_op jit(solution)/shard_map/all_to_all | solution.py:377
  55.8 20.6 %window_attention.1 = (bf16[8,128,128]{2,1,0:T(8,128)(2,1)S(1)}, bf16[8,128,128]{2,1,0:T(8,128)(2,1)S(1)}, bf16[8,128,128]{2,1,0:T(8,128)(2,1)S(1)}, bf16[8,128,128]{2,1,0:T(8,128)(2,1)S(1)}) custom-call(s32[4]{0:T(128)S(1)} %pad_add_fusion.ids_ref, bf16[32,128,128]{2,1,0:T(8,128)(2,1)} %all-to-all-done.x_ref), custom_call_target="tpu_custom_call" | custom-call | flops 2013265920 | bytes 2097168 | tf_op jit(solution)/shard_map/window_attention/pallas_call | solution.py:166
  76.5 1.2 collective-permute-start
  77.7 2.6 %collective-permute-start.1 = (bf16[8,128,128]{2,1,0:T(8,128)(2,1)S(1)}, bf16[8,128,128]{2,1,0:T(8,128)(2,1)S(1)}, u32[]{:S(2)}, u32[]{:S(2)}) collective-permute-start(bf16[8,128,128]{2,1,0:T(8,128)(2,1)S(1)} %get-tuple-element.19), channel_id=1, source_target_pairs={{0,16},{8,24},{16,0},{24,8},{1,17},{9,25},{17,1},{25,9},{2,18},{10... | collective-permute-start | bytes 786440 | tf_op jit(solution)/shard_map/ppermute | solution.py:323
  80.3 1.1 collective-permute-start.2
  81.4 2.0 %collective-permute-done.refs_1_ = bf16[8,128,128]{2,1,0:T(8,128)(2,1)S(1)} collective-permute-done((bf16[8,128,128]{2,1,0:T(8,128)(2,1)S(1)}, bf16[8,128,128]{2,1,0:T(8,128)(2,1)S(1)}, u32[]{:S(2)}, u32[]{:S(2)}) %collective-permute-start) | collective-permute-done | bytes 262176 | tf_op jit(solution)/shard_map/ppermute | solution.py:323
  83.4 3.6 %collective-permute-done.1.refs_2_ = bf16[8,128,128]{2,1,0:T(8,128)(2,1)S(1)} collective-permute-done((bf16[8,128,128]{2,1,0:T(8,128)(2,1)S(1)}, bf16[8,128,128]{2,1,0:T(8,128)(2,1)S(1)}, u32[]{:S(2)}, u32[]{:S(2)}) %collective-permute-start.1) | collective-permute-done | bytes 262176 | tf_op jit(solution)/shard_map/ppermute | solution.py:323
  87.0 1.2 input_terms.1
  88.3 1.4 copy-done.1
  89.7 0.9 all-gather.3.cloned.1.call-done
  90.6 0.1 copy-done.7
  90.7 2.2 %copy-done.3 = bf16[16384,128]{1,0:T(8,128)(2,1)S(1)} copy-done((bf16[16384,128]{1,0:T(8,128)(2,1)S(1)}, bf16[16384,128]{1,0:T(8,128)(2,1)}, u32[]{:S(2)}) %copy-start.3) | copy-done | bytes 4194328
  92.9 2.1 %weight_grad_terms.1 = (bf16[4,512,128]{2,1,0:T(8,128)(2,1)S(1)}, bf16[4,512,128]{2,1,0:T(8,128)(2,1)S(1)}) custom-call(s32[4]{0:T(128)S(1)} %pad_add_fusion.ids_ref, bf16[8,128,128]{2,1,0:T(8,128)(2,1)S(1)} %get-tuple-element.17.refs_0_, bf16[8,128,128]{2,1,0:T(8,128)(2,1)S(1)} %collective-permute-done.refs_1_, bf16[8,128,128]{2,1,0:T(8,128)(2,1)S(1)} %copy-done.5, ...), custom_call_target="tpu_custom_call" | custom-call | flops 1073741824 | bytes 6291472 | tf_op jit(solution)/shard_map/weight_grad_terms/pallas_call | solution.py:166
  95.0 7.2 %collective-permute-start.3 = (bf16[4,512,128]{2,1,0:T(8,128)(2,1)S(1)}, bf16[4,512,128]{2,1,0:T(8,128)(2,1)S(1)}, u32[]{:S(2)}, u32[]{:S(2)}) collective-permute-start(bf16[4,512,128]{2,1,0:T(8,128)(2,1)S(1)} %get-tuple-element.24), channel_id=1, source_target_pairs={{0,32},{32,0},{1,33},{33,1},{2,34},{34,2},{3,35},{35,3},{4,36},{36... | collective-permute-start | bytes 1572872 | tf_op jit(solution)/shard_map/ppermute | solution.py:318
  102.2 1.5 collective-permute-done.3
  103.7 0.1 add_convert_fusion
  103.9 2.7 %collective-permute-start.6 = (bf16[512,128]{1,0:T(8,128)(2,1)S(1)}, bf16[512,128]{1,0:T(8,128)(2,1)S(1)}, u32[]{:S(2)}, u32[]{:S(2)}) collective-permute-start(bf16[512,128]{1,0:T(8,128)(2,1)S(1)} %get-tuple-element.28), channel_id=1, source_target_pairs={{0,24},{8,0},{16,8},{24,16},{1,25},{9,1},{17,9},{25,17},{2,26},{10... | collective-permute-start | bytes 393224 | tf_op jit(solution)/shard_map/ppermute | solution.py:323
  106.5 1.4 collective-permute-start.4
  107.9 1.3 collective-permute-done.6
  109.2 6.2 %collective-permute-done.5 = bf16[512,128]{1,0:T(8,128)(2,1)S(1)} collective-permute-done((bf16[512,128]{1,0:T(8,128)(2,1)S(1)}, bf16[512,128]{1,0:T(8,128)(2,1)S(1)}, u32[]{:S(2)}, u32[]{:S(2)}) %collective-permute-start.5) | collective-permute-done | bytes 131104 | tf_op jit(solution)/shard_map/ppermute | solution.py:323
  115.4 0.1 fusion.1
  115.5 1.3 collective-permute-start.7
  116.8 3.0 %collective-permute-done.7 = bf16[512,128]{1,0:T(8,128)(2,1)S(1)} collective-permute-done((bf16[512,128]{1,0:T(8,128)(2,1)S(1)}, bf16[512,128]{1,0:T(8,128)(2,1)S(1)}, u32[]{:S(2)}, u32[]{:S(2)}) %collective-permute-start.7) | collective-permute-done | bytes 131104 | tf_op jit(solution)/shard_map/ppermute | solution.py:334
  119.8 3.1 %collective-permute-start.8 = (bf16[512,128]{1,0:T(8,128)(2,1)S(1)}, bf16[512,128]{1,0:T(8,128)(2,1)S(1)}, u32[]{:S(2)}, u32[]{:S(2)}) collective-permute-start(bf16[512,128]{1,0:T(8,128)(2,1)S(1)} %add_convert_fusion.2), channel_id=1, source_target_pairs={{0,192},{192,0},{64,128},{128,64},{1,193},{193,1},{65,129},{129,65... | collective-permute-start | bytes 393224 | tf_op jit(solution)/shard_map/ppermute | solution.py:335
  122.9 2.7 %collective-permute-done.8 = bf16[512,128]{1,0:T(8,128)(2,1)S(1)} collective-permute-done((bf16[512,128]{1,0:T(8,128)(2,1)S(1)}, bf16[512,128]{1,0:T(8,128)(2,1)S(1)}, u32[]{:S(2)}, u32[]{:S(2)}) %collective-permute-start.8) | collective-permute-done | bytes 131104 | tf_op jit(solution)/shard_map/ppermute | solution.py:335
  125.7 2.4 %collective-permute-start.9 = (bf16[384,128]{1,0:T(8,128)(2,1)S(1)}, bf16[384,128]{1,0:T(8,128)(2,1)S(1)}, u32[]{:S(2)}, u32[]{:S(2)}) collective-permute-start(bf16[384,128]{1,0:T(8,128)(2,1)S(1)} %slice.29), channel_id=1, source_target_pairs={{0,32},{32,0},{1,33},{33,1},{2,34},{34,2},{3,35},{35,3},{4,36},{36... | collective-permute-start | bytes 294920 | tf_op jit(solution)/shard_map/ppermute | solution.py:318
  128.1 0.6 slice.28
  128.7 8.0 %all-to-all-start.1 = ((bf16[8,16,128]{2,1,0:T(8,128)(2,1)}), bf16[8,16,128]{2,1,0:T(8,128)(2,1)S(1)}, u32[]{:S(2)}, u32[]{:S(2)}) async-start(bf16[8,16,128]{2,1,0:T(8,128)(2,1)} %bitcast.16), calls=%async_computation.2 | async-start | bytes 65536 | tf_op jit(solution)/shard_map/all_to_all | solution.py:351
  136.7 0.3 copy.12
  137.0 0.9 reshape.51
  137.9 5.6 %all-to-all-done.1 = bf16[8,16,128]{2,1,0:T(8,128)(2,1)S(1)} async-done(((bf16[8,16,128]{2,1,0:T(8,128)(2,1)}), bf16[8,16,128]{2,1,0:T(8,128)(2,1)S(1)}, u32[]{:S(2)}, u32[]{:S(2)}) %all-to-all-start.1) | async-done | bytes 32800 | tf_op jit(solution)/shard_map/all_to_all | solution.py:351
  143.5 1.4 collective-permute-start.10
  145.0 0.1 stack.49
  145.1 0.1 copy.13
  145.2 0.6 collective-permute-done.10
  145.8 0.1 stack.50
  145.9 0.1 copy.14
  146.0 0.1 convert_bitcast_fusion
  146.2 0.9 reshape.52
  (34 shorter events, 0.3 us)
Async XLA Ops:
  7.2 1.6 %copy-start = (bf16[1024,1024]{1,0:T(8,128)(2,1)S(1)}, bf16[1024,1024]{1,0:T(8,128)(2,1)}, u32[]{:S(2)}) copy-start(bf16[1024,1024]{1,0:T(8,128)(2,1)} %param.15) | copy-start | bytes 6291460
  7.2 3.3 %copy-start.10 = (bf16[1,1024,128]{2,1,0:T(8,128)(2,1)S(1)}, bf16[1,1024,128]{2,1,0:T(8,128)(2,1)}, u32[]{:S(2)}) copy-start(bf16[1,1024,128]{2,1,0:T(8,128)(2,1)} %param.12) | copy-start | bytes 786436
  7.2 3.3 %copy-start.11 = (bf16[1,1024,128]{2,1,0:T(8,128)(2,1)S(1)}, bf16[1,1024,128]{2,1,0:T(8,128)(2,1)}, u32[]{:S(2)}) copy-start(bf16[1,1024,128]{2,1,0:T(8,128)(2,1)} %param.11) | copy-start | bytes 786436
  7.2 3.3 %copy-start.12 = (bf16[1,1024,128]{2,1,0:T(8,128)(2,1)S(1)}, bf16[1,1024,128]{2,1,0:T(8,128)(2,1)}, u32[]{:S(2)}) copy-start(bf16[1,1024,128]{2,1,0:T(8,128)(2,1)} %param.10) | copy-start | bytes 786436
  7.2 83.4 %all-gather.3.cloned.1.call-start = ((), (), s32[]{:S(2)}) async-start(), calls=%async_computation.4 | async-start | bytes 4718592 | tf_op jit(solution)/shard_map/all_gather | solution.py:379
  10.5 1.2 copy-start.8
  10.5 1.2 copy-start.9
  12.6 43.3 %all-to-all-start = ((bf16[32,128,128]{2,1,0:T(8,128)(2,1)}), bf16[32,128,128]{2,1,0:T(8,128)(2,1)}, u32[]{:S(2)}, u32[]{:S(2)}) async-start(bf16[32,128,128]{2,1,0:T(8,128)(2,1)} %pad_maximum_fusion), calls=%async_computation | async-start | bytes 2097152 | tf_op jit(solution)/shard_map/all_to_all | solution.py:377
  24.6 122.5 %reduce-scatter.2.cloned.1.call-start = ((), (), s32[]{:S(2)}) async-start(), calls=%async_computation.3 | async-start | bytes 2359296 | tf_op jit(solution)/shard_map/reduce_scatter | solution.py:385
  26.0 3.0 %copy-start.2 = (bf16[1024,3072]{1,0:T(8,128)(2,1)S(1)}, bf16[1024,3072]{1,0:T(8,128)(2,1)}, u32[]{:S(2)}) copy-start(bf16[1024,3072]{1,0:T(8,128)(2,1)} %w_ref.1) | copy-start | bytes 18874372
  76.5 6.9 %collective-permute-start = (bf16[8,128,128]{2,1,0:T(8,128)(2,1)S(1)}, bf16[8,128,128]{2,1,0:T(8,128)(2,1)S(1)}, u32[]{:S(2)}, u32[]{:S(2)}) collective-permute-start(bf16[8,128,128]{2,1,0:T(8,128)(2,1)S(1)} %get-tuple-element.18), channel_id=1, source_target_pairs={{0,8},{8,16},{16,24},{24,0},{1,9},{9,17},{17,25},{25,1},{2,10},{10... | collective-permute-start | bytes 786440 | tf_op jit(solution)/shard_map/ppermute | solution.py:323
  77.7 9.3 %collective-permute-start.1 = (bf16[8,128,128]{2,1,0:T(8,128)(2,1)S(1)}, bf16[8,128,128]{2,1,0:T(8,128)(2,1)S(1)}, u32[]{:S(2)}, u32[]{:S(2)}) collective-permute-start(bf16[8,128,128]{2,1,0:T(8,128)(2,1)S(1)} %get-tuple-element.19), channel_id=1, source_target_pairs={{0,16},{8,24},{16,0},{24,8},{1,17},{9,25},{17,1},{25,9},{2,18},{10... | collective-permute-start | bytes 786440 | tf_op jit(solution)/shard_map/ppermute | solution.py:323
  80.3 6.7 %collective-permute-start.2 = (bf16[8,128,128]{2,1,0:T(8,128)(2,1)S(1)}, bf16[8,128,128]{2,1,0:T(8,128)(2,1)S(1)}, u32[]{:S(2)}, u32[]{:S(2)}) collective-permute-start(bf16[8,128,128]{2,1,0:T(8,128)(2,1)S(1)} %get-tuple-element.20), channel_id=1, source_target_pairs={{0,24},{8,0},{16,8},{24,16},{1,25},{9,1},{17,9},{25,17},{2,26},{10... | collective-permute-start | bytes 786440 | tf_op jit(solution)/shard_map/ppermute | solution.py:323
  87.0 1.3 copy-start.4
  87.0 1.3 copy-start.6
  88.3 1.4 copy-start.1
  89.6 1.0 copy-start.5
  89.6 1.0 copy-start.7
  90.7 2.2 %copy-start.3 = (bf16[16384,128]{1,0:T(8,128)(2,1)S(1)}, bf16[16384,128]{1,0:T(8,128)(2,1)}, u32[]{:S(2)}) copy-start(bf16[16384,128]{1,0:T(8,128)(2,1)} %all-gather.3.cloned.1.call-done) | copy-start | bytes 12582916
  95.0 8.7 %collective-permute-start.3 = (bf16[4,512,128]{2,1,0:T(8,128)(2,1)S(1)}, bf16[4,512,128]{2,1,0:T(8,128)(2,1)S(1)}, u32[]{:S(2)}, u32[]{:S(2)}) collective-permute-start(bf16[4,512,128]{2,1,0:T(8,128)(2,1)S(1)} %get-tuple-element.24), channel_id=1, source_target_pairs={{0,32},{32,0},{1,33},{33,1},{2,34},{34,2},{3,35},{35,3},{4,36},{36... | collective-permute-start | bytes 1572872 | tf_op jit(solution)/shard_map/ppermute | solution.py:318
  103.9 5.4 %collective-permute-start.6 = (bf16[512,128]{1,0:T(8,128)(2,1)S(1)}, bf16[512,128]{1,0:T(8,128)(2,1)S(1)}, u32[]{:S(2)}, u32[]{:S(2)}) collective-permute-start(bf16[512,128]{1,0:T(8,128)(2,1)S(1)} %get-tuple-element.28), channel_id=1, source_target_pairs={{0,24},{8,0},{16,8},{24,16},{1,25},{9,1},{17,9},{25,17},{2,26},{10... | collective-permute-start | bytes 393224 | tf_op jit(solution)/shard_map/ppermute | solution.py:323
  106.5 8.9 %collective-permute-start.5 = (bf16[512,128]{1,0:T(8,128)(2,1)S(1)}, bf16[512,128]{1,0:T(8,128)(2,1)S(1)}, u32[]{:S(2)}, u32[]{:S(2)}) collective-permute-start(bf16[512,128]{1,0:T(8,128)(2,1)S(1)} %get-tuple-element.29), channel_id=1, source_target_pairs={{0,8},{8,16},{16,24},{24,0},{1,9},{9,17},{17,25},{25,1},{2,10},{10... | collective-permute-start | bytes 393224 | tf_op jit(solution)/shard_map/ppermute | solution.py:323
  106.5 8.9 %collective-permute-start.4 = (bf16[512,128]{1,0:T(8,128)(2,1)S(1)}, bf16[512,128]{1,0:T(8,128)(2,1)S(1)}, u32[]{:S(2)}, u32[]{:S(2)}) collective-permute-start(bf16[512,128]{1,0:T(8,128)(2,1)S(1)} %get-tuple-element.27), channel_id=1, source_target_pairs={{0,16},{8,24},{16,0},{24,8},{1,17},{9,25},{17,1},{25,9},{2,18},{10... | collective-permute-start | bytes 393224 | tf_op jit(solution)/shard_map/ppermute | solution.py:323
  115.5 4.3 %collective-permute-start.7 = (bf16[512,128]{1,0:T(8,128)(2,1)S(1)}, bf16[512,128]{1,0:T(8,128)(2,1)S(1)}, u32[]{:S(2)}, u32[]{:S(2)}) collective-permute-start(bf16[512,128]{1,0:T(8,128)(2,1)S(1)} %fusion.1), channel_id=1, source_target_pairs={{0,64},{64,0},{128,192},{192,128},{1,65},{65,1},{129,193},{193,129... | collective-permute-start | bytes 393224 | tf_op jit(solution)/shard_map/ppermute | solution.py:334
  119.8 5.8 %collective-permute-start.8 = (bf16[512,128]{1,0:T(8,128)(2,1)S(1)}, bf16[512,128]{1,0:T(8,128)(2,1)S(1)}, u32[]{:S(2)}, u32[]{:S(2)}) collective-permute-start(bf16[512,128]{1,0:T(8,128)(2,1)S(1)} %add_convert_fusion.2), channel_id=1, source_target_pairs={{0,192},{192,0},{64,128},{128,64},{1,193},{193,1},{65,129},{129,65... | collective-permute-start | bytes 393224 | tf_op jit(solution)/shard_map/ppermute | solution.py:335
  125.7 11.0 %collective-permute-start.9 = (bf16[384,128]{1,0:T(8,128)(2,1)S(1)}, bf16[384,128]{1,0:T(8,128)(2,1)S(1)}, u32[]{:S(2)}, u32[]{:S(2)}) collective-permute-start(bf16[384,128]{1,0:T(8,128)(2,1)S(1)} %slice.29), channel_id=1, source_target_pairs={{0,32},{32,0},{1,33},{33,1},{2,34},{34,2},{3,35},{35,3},{4,36},{36... | collective-permute-start | bytes 294920 | tf_op jit(solution)/shard_map/ppermute | solution.py:318
  128.7 14.8 %all-to-all-start.1 = ((bf16[8,16,128]{2,1,0:T(8,128)(2,1)}), bf16[8,16,128]{2,1,0:T(8,128)(2,1)S(1)}, u32[]{:S(2)}, u32[]{:S(2)}) async-start(bf16[8,16,128]{2,1,0:T(8,128)(2,1)} %bitcast.16), calls=%async_computation.2 | async-start | bytes 65536 | tf_op jit(solution)/shard_map/all_to_all | solution.py:351
  143.5 2.3 %collective-permute-start.10 = (bf16[8,16,128]{2,1,0:T(8,128)(2,1)S(1)}, bf16[8,16,128]{2,1,0:T(8,128)(2,1)S(1)}, u32[]{:S(2)}, u32[]{:S(2)}) collective-permute-start(bf16[8,16,128]{2,1,0:T(8,128)(2,1)S(1)} %all-to-all-done.1), channel_id=1, source_target_pairs={{0,32},{32,0},{1,33},{33,1},{2,34},{34,2},{3,35},{35,3},{4,36},{36... | collective-permute-start | bytes 98312 | tf_op jit(solution)/shard_map/ppermute | solution.py:318
Sparse Core Ops, SparseCore 0:
  12.7 77.8 all-gather.2
  93.7 43.2 reduce-scatter.1

commit v4 on v3

--- a/solution.py
+++ b/solution.py
@@ -23,6 +23,10 @@
     parts, (gq_ref, ao_ref, kv_t, k_p, v_p, acc) = refs[:-6], refs[-6:]
     nx, nz = len(parts), parts[0].shape[0]
     own_x = ids_ref[1]
+
+    def at(b):
+        return lax.rem(b, nz) * nx + b // nz
+
     blocks = x_ref.shape[0]
     seq = blocks * BLK
     span = QT + 2 * HALF
@@ -44,8 +48,8 @@
 
     def prep(b, _):
         start = pl.multiple_of(HALF + b * BLK, BLK)
-        k_blk = x_ref[b, HEAD_DIM : 2 * HEAD_DIM, :]
-        v_blk = x_ref[b, 2 * HEAD_DIM : 3 * HEAD_DIM, :]
+        k_blk = x_ref[at(b), HEAD_DIM : 2 * HEAD_DIM, :]
+        v_blk = x_ref[at(b), 2 * HEAD_DIM : 3 * HEAD_DIM, :]
         k_p[:, pl.ds(start, BLK)] = k_blk
         v_p[:, pl.ds(start, BLK)] = v_blk
         bias = jnp.where((row_id == 0) & (row_frame + b * BLK >= live), masked_score, 0.0)
@@ -75,7 +79,7 @@
         bases = [pl.multiple_of(i * QT, QT) for i in tiles]
         qs, gs = [], []
         for i in tiles:
-            x0, x1 = x_ref[2 * i], x_ref[2 * i + 1]
+            x0, x1 = x_ref[at(2 * i)], x_ref[at(2 * i + 1)]
             q = jnp.concatenate([x0[0:32], x1[0:32]], axis=1)
             g = jnp.concatenate([x0[96:128], x1[96:128]], axis=1)
             qs.append(jnp.concatenate([q, ones_row, z64], axis=0))
@@ -371,10 +375,11 @@
         w_out, own_grad, (((0,), (0,)), ((), ())), preferred_element_type=f32
     ).astype(bf)
     sent = jnp.concatenate(
-        [a.reshape(shards, HEAD_DIM, frames) for a in (query_act[0], key_act[0], value_act[0], head_grad)],
-        axis=1,
+        [a.reshape(nx, nz, HEAD_DIM, frames) for a in (query_act[0], key_act[0], value_act[0], head_grad)],
+        axis=2,
     )
-    heads = lax.all_to_all(sent, FRAME_AXES, 0, 0, tiled=True)
+    sent = sent.transpose(1, 0, 2, 3).reshape(shards, 4 * HEAD_DIM, frames)
+    heads = lax.all_to_all(sent, ("z", "x"), 0, 0, tiled=True)
     own, _ = lax.optimization_barrier(((normed[0], own_grad), sent))
     gathered = lax.all_gather(jnp.concatenate(own, axis=0), "z")
     weights = own_weights(ids, w_qkv, nx)

time: 154 us -> 153 us (level)
  starting transfers between devices: 44.5 us -> 40.3 us
  local copies, waits for them, and re-layouts: 11.2 us -> 13.3 us
  waiting for transfers between devices: 52.5 us -> 54.6 us
    all_to_all x1, starting transfers between devices: 8 us -> 3.43 us  [weight_grads(): out = lax.all_to_all(out, 'z', 0, 0, tiled=True)]
    all_to_all x1, waiting for transfers between devices: 25 us -> 28.7 us  [body(): heads = lax.all_to_all(sent, ('z', 'x'), 0, 0, tiled=True)]
where the time goes in v4:
time: 153 us
  waiting for transfers between devices  54.6 us (36%)
  starting transfers between devices  40.3 us (26%)
  Pallas kernels  25.9 us (17%)
  between operations  15.6 us (10%)
  local copies, waits for them, and re-layouts  13.3 us (9%)
  matrix products  1.71 us (1%)
    all_to_all x1, waiting for transfers between devices, body(): heads = lax.all_to_all(sent, ('z', 'x'), 0, 0, tiled=True)  28.7 us
    pallas_call x4, Pallas kernels, kernel_call(): pl.pallas_call(kernel, out_shape=outs, in_specs=[pl.BlockSpec(memory_spac...  25.9 us
    ppermute x6, waiting for transfers between devices, shift(): return lax.ppermute(v, axis, [(i, (i + k) % n) for i in range(n)])  12.8 us
    all_to_all x1, starting transfers between devices, body(): heads = lax.all_to_all(sent, ('z', 'x'), 0, 0, tiled=True)  12 us
    ppermute x3, starting transfers between devices, swap_cores(): return lax.ppermute(v, 'core', [(0, 1), (1, 0)])  10.2 us
    ppermute x6, starting transfers between devices, shift(): return lax.ppermute(v, axis, [(i, (i + k) % n) for i in range(n)])  9.95 us
    unnamed x26, local copies, waits for them, and re-layouts  9.04 us
    all_to_all x1, waiting for transfers between devices, weight_grads(): out = lax.all_to_all(out, 'z', 0, 0, tiled=True)  5.62 us
  transfers between devices with their start and end apart: 15, of which 11 were waited for; matrix products, arithmetic and copies ran while one was open for 2% of the time, Pallas kernels for 17%

profile of v4, /device:TPU:1, one launch (start us, length us, event | category | flops | bytes accessed | tf_op | source)
XLA Modules:
  0.0 152.8 jit_solution(6946388439257860766)
XLA Ops:
  7.3 1.5 copy-done
  8.8 1.7 %convolution_convert_fusion = bf16[1024,128]{1,0:T(8,128)(2,1)S(1)} fusion(bf16[1024,1024]{1,0:T(8,128)(2,1)S(1)} %copy-done, bf16[1,1024,128]{2,1,0:T(8,128)(2,1)} %param.13), kind=kOutput, calls=%fused_computation | convolution fusion | flops 268566528 | bytes 2621440 | tf_op jit(solution)/shard_map/dot_general | solution.py:374
  10.5 0.1 pad_maximum_fusion
  10.7 1.1 copy.21
  11.8 0.8 pad_maximum_fusion.1
  12.6 12.0 %all-to-all-start = ((bf16[32,128,128]{2,1,0:T(8,128)(2,1)}), bf16[32,128,128]{2,1,0:T(8,128)(2,1)}, u32[]{:S(2)}, u32[]{:S(2)}) async-start(bf16[32,128,128]{2,1,0:T(8,128)(2,1)} %bitcast.6), calls=%async_computation | async-start | bytes 2097152 | tf_op jit(solution)/shard_map/all_to_all | solution.py:382
  26.0 0.1 pad_add_fusion.ids_ref
  26.1 3.0 %copy-done.2 = bf16[1024,3072]{1,0:T(8,128)(2,1)S(1)} copy-done((bf16[1024,3072]{1,0:T(8,128)(2,1)S(1)}, bf16[1024,3072]{1,0:T(8,128)(2,1)}, u32[]{:S(2)}) %copy-start.2) | copy-done | bytes 6291480
  29.1 1.9 %own_weights.1.weights_ref = bf16[1024,384]{1,0:T(8,128)(2,1)S(1)} custom-call(s32[4]{0:T(128)S(1)} %pad_add_fusion.ids_ref, bf16[1024,3072]{1,0:T(8,128)(2,1)S(1)} %copy-done.2), custom_call_target="tpu_custom_call" | custom-call | bytes 7077904 | tf_op jit(solution)/shard_map/own_weights/pallas_call | solution.py:170
  30.9 28.7 %all-to-all-done.x_ref = bf16[32,128,128]{2,1,0:T(8,128)(2,1)} async-done(((bf16[32,128,128]{2,1,0:T(8,128)(2,1)}), bf16[32,128,128]{2,1,0:T(8,128)(2,1)}, u32[]{:S(2)}, u32[]{:S(2)}) %all-to-all-start) | async-done | bytes 1048608 | tf_op jit(solution)/shard_map/all_to_all | solution.py:382
  59.6 20.6 %window_attention.1 = (bf16[8,128,128]{2,1,0:T(8,128)(2,1)S(1)}, bf16[8,128,128]{2,1,0:T(8,128)(2,1)S(1)}, bf16[8,128,128]{2,1,0:T(8,128)(2,1)S(1)}, bf16[8,128,128]{2,1,0:T(8,128)(2,1)S(1)}) custom-call(s32[4]{0:T(128)S(1)} %pad_add_fusion.ids_ref, bf16[32,128,128]{2,1,0:T(8,128)(2,1)} %all-to-all-done.x_ref), custom_call_target="tpu_custom_call" | custom-call | flops 2013265920 | bytes 2097168 | tf_op jit(solution)/shard_map/window_attention/pallas_call | solution.py:170
  80.3 2.8 %collective-permute-start = (bf16[8,128,128]{2,1,0:T(8,128)(2,1)S(1)}, bf16[8,128,128]{2,1,0:T(8,128)(2,1)S(1)}, u32[]{:S(2)}, u32[]{:S(2)}) collective-permute-start(bf16[8,128,128]{2,1,0:T(8,128)(2,1)S(1)} %get-tuple-element.18), channel_id=1, source_target_pairs={{0,8},{8,16},{16,24},{24,0},{1,9},{9,17},{17,25},{25,1},{2,10},{10... | collective-permute-start | bytes 786440 | tf_op jit(solution)/shard_map/ppermute | solution.py:327
  83.1 2.1 %collective-permute-start.1 = (bf16[8,128,128]{2,1,0:T(8,128)(2,1)S(1)}, bf16[8,128,128]{2,1,0:T(8,128)(2,1)S(1)}, u32[]{:S(2)}, u32[]{:S(2)}) collective-permute-start(bf16[8,128,128]{2,1,0:T(8,128)(2,1)S(1)} %get-tuple-element.19), channel_id=1, source_target_pairs={{0,16},{8,24},{16,0},{24,8},{1,17},{9,25},{17,1},{25,9},{2,18},{10... | collective-permute-start | bytes 786440 | tf_op jit(solution)/shard_map/ppermute | solution.py:327
  85.2 1.0 collective-permute-start.2
  86.2 2.0 %collective-permute-done.refs_1_ = bf16[8,128,128]{2,1,0:T(8,128)(2,1)S(1)} collective-permute-done((bf16[8,128,128]{2,1,0:T(8,128)(2,1)S(1)}, bf16[8,128,128]{2,1,0:T(8,128)(2,1)S(1)}, u32[]{:S(2)}, u32[]{:S(2)}) %collective-permute-start) | collective-permute-done | bytes 262176 | tf_op jit(solution)/shard_map/ppermute | solution.py:327
  88.2 5.1 %collective-permute-done.1.refs_2_ = bf16[8,128,128]{2,1,0:T(8,128)(2,1)S(1)} collective-permute-done((bf16[8,128,128]{2,1,0:T(8,128)(2,1)S(1)}, bf16[8,128,128]{2,1,0:T(8,128)(2,1)S(1)}, u32[]{:S(2)}, u32[]{:S(2)}) %collective-permute-start.1) | collective-permute-done | bytes 262176 | tf_op jit(solution)/shard_map/ppermute | solution.py:327
  93.3 1.3 input_terms.1
  94.6 1.4 copy-done.1
  96.0 0.9 copy-done.5
  96.9 0.1 copy-done.7
  97.0 2.2 %copy-done.3 = bf16[16384,128]{1,0:T(8,128)(2,1)S(1)} copy-done((bf16[16384,128]{1,0:T(8,128)(2,1)S(1)}, bf16[16384,128]{1,0:T(8,128)(2,1)}, u32[]{:S(2)}) %copy-start.3) | copy-done | bytes 4194328
  99.1 2.1 %weight_grad_terms.1 = (bf16[4,512,128]{2,1,0:T(8,128)(2,1)S(1)}, bf16[4,512,128]{2,1,0:T(8,128)(2,1)S(1)}) custom-call(s32[4]{0:T(128)S(1)} %pad_add_fusion.ids_ref, bf16[8,128,128]{2,1,0:T(8,128)(2,1)S(1)} %get-tuple-element.17.refs_0_, bf16[8,128,128]{2,1,0:T(8,128)(2,1)S(1)} %collective-permute-done.refs_1_, bf16[8,128,128]{2,1,0:T(8,128)(2,1)S(1)} %copy-done.5, ...), custom_call_target="tpu_custom_call" | custom-call | flops 1073741824 | bytes 6291472 | tf_op jit(solution)/shard_map/weight_grad_terms/pallas_call | solution.py:170
  101.2 4.9 %collective-permute-start.3 = (bf16[4,512,128]{2,1,0:T(8,128)(2,1)S(1)}, bf16[4,512,128]{2,1,0:T(8,128)(2,1)S(1)}, u32[]{:S(2)}, u32[]{:S(2)}) collective-permute-start(bf16[4,512,128]{2,1,0:T(8,128)(2,1)S(1)} %get-tuple-element.24), channel_id=1, source_target_pairs={{0,32},{32,0},{1,33},{33,1},{2,34},{34,2},{3,35},{35,3},{4,36},{36... | collective-permute-start | bytes 1572872 | tf_op jit(solution)/shard_map/ppermute | solution.py:322
  106.1 1.5 %collective-permute-done.3 = bf16[4,512,128]{2,1,0:T(8,128)(2,1)S(1)} collective-permute-done((bf16[4,512,128]{2,1,0:T(8,128)(2,1)S(1)}, bf16[4,512,128]{2,1,0:T(8,128)(2,1)S(1)}, u32[]{:S(2)}, u32[]{:S(2)}) %collective-permute-start.3) | collective-permute-done | bytes 524320 | tf_op jit(solution)/shard_map/ppermute | solution.py:322
  107.7 0.1 add_convert_fusion
  107.8 2.1 %collective-permute-start.6 = (bf16[512,128]{1,0:T(8,128)(2,1)S(1)}, bf16[512,128]{1,0:T(8,128)(2,1)S(1)}, u32[]{:S(2)}, u32[]{:S(2)}) collective-permute-start(bf16[512,128]{1,0:T(8,128)(2,1)S(1)} %get-tuple-element.28), channel_id=1, source_target_pairs={{0,24},{8,0},{16,8},{24,16},{1,25},{9,1},{17,9},{25,17},{2,26},{10... | collective-permute-start | bytes 393224 | tf_op jit(solution)/shard_map/ppermute | solution.py:327
  110.0 1.9 %collective-permute-start.4 = (bf16[512,128]{1,0:T(8,128)(2,1)S(1)}, bf16[512,128]{1,0:T(8,128)(2,1)S(1)}, u32[]{:S(2)}, u32[]{:S(2)}) collective-permute-start(bf16[512,128]{1,0:T(8,128)(2,1)S(1)} %get-tuple-element.27), channel_id=1, source_target_pairs={{0,16},{8,24},{16,0},{24,8},{1,17},{9,25},{17,1},{25,9},{2,18},{10... | collective-permute-start | bytes 393224 | tf_op jit(solution)/shard_map/ppermute | solution.py:327
  111.9 1.0 collective-permute-done.6
  112.9 3.7 %collective-permute-done.5 = bf16[512,128]{1,0:T(8,128)(2,1)S(1)} collective-permute-done((bf16[512,128]{1,0:T(8,128)(2,1)S(1)}, bf16[512,128]{1,0:T(8,128)(2,1)S(1)}, u32[]{:S(2)}, u32[]{:S(2)}) %collective-permute-start.5) | collective-permute-done | bytes 131104 | tf_op jit(solution)/shard_map/ppermute | solution.py:327
  116.6 1.0 collective-permute-done.4
  117.7 1.4 collective-permute-start.7
  119.1 2.9 %collective-permute-done.7 = bf16[512,128]{1,0:T(8,128)(2,1)S(1)} collective-permute-done((bf16[512,128]{1,0:T(8,128)(2,1)S(1)}, bf16[512,128]{1,0:T(8,128)(2,1)S(1)}, u32[]{:S(2)}, u32[]{:S(2)}) %collective-permute-start.7) | collective-permute-done | bytes 131104 | tf_op jit(solution)/shard_map/ppermute | solution.py:338
  122.0 3.2 %collective-permute-start.8 = (bf16[512,128]{1,0:T(8,128)(2,1)S(1)}, bf16[512,128]{1,0:T(8,128)(2,1)S(1)}, u32[]{:S(2)}, u32[]{:S(2)}) collective-permute-start(bf16[512,128]{1,0:T(8,128)(2,1)S(1)} %add_convert_fusion.2), channel_id=1, source_target_pairs={{0,192},{192,0},{64,128},{128,64},{1,193},{193,1},{65,129},{129,65... | collective-permute-start | bytes 393224 | tf_op jit(solution)/shard_map/ppermute | solution.py:339
  125.2 2.4 %collective-permute-done.8 = bf16[512,128]{1,0:T(8,128)(2,1)S(1)} collective-permute-done((bf16[512,128]{1,0:T(8,128)(2,1)S(1)}, bf16[512,128]{1,0:T(8,128)(2,1)S(1)}, u32[]{:S(2)}, u32[]{:S(2)}) %collective-permute-start.8) | collective-permute-done | bytes 131104 | tf_op jit(solution)/shard_map/ppermute | solution.py:339
  127.6 3.9 %collective-permute-start.9 = (bf16[384,128]{1,0:T(8,128)(2,1)S(1)}, bf16[384,128]{1,0:T(8,128)(2,1)S(1)}, u32[]{:S(2)}, u32[]{:S(2)}) collective-permute-start(bf16[384,128]{1,0:T(8,128)(2,1)S(1)} %slice.29), channel_id=1, source_target_pairs={{0,32},{32,0},{1,33},{33,1},{2,34},{34,2},{3,35},{35,3},{4,36},{36... | collective-permute-start | bytes 294920 | tf_op jit(solution)/shard_map/ppermute | solution.py:322
  131.5 0.6 slice.28
  132.1 3.4 %all-to-all-start.1 = ((bf16[8,16,128]{2,1,0:T(8,128)(2,1)}), bf16[8,16,128]{2,1,0:T(8,128)(2,1)S(1)}, u32[]{:S(2)}, u32[]{:S(2)}) async-start(bf16[8,16,128]{2,1,0:T(8,128)(2,1)} %bitcast.19), calls=%async_computation.2 | async-start | bytes 65536 | tf_op jit(solution)/shard_map/all_to_all | solution.py:355
  135.6 0.3 copy.16
  135.9 0.9 reshape.55
  136.8 5.6 %all-to-all-done.1 = bf16[8,16,128]{2,1,0:T(8,128)(2,1)S(1)} async-done(((bf16[8,16,128]{2,1,0:T(8,128)(2,1)}), bf16[8,16,128]{2,1,0:T(8,128)(2,1)S(1)}, u32[]{:S(2)}, u32[]{:S(2)}) %all-to-all-start.1) | async-done | bytes 32800 | tf_op jit(solution)/shard_map/all_to_all | solution.py:355
  142.4 1.5 collective-permute-start.10
  143.9 0.1 stack.49
  144.0 0.1 copy.17
  144.1 0.6 collective-permute-done.10
  144.7 0.1 stack.50
  144.9 0.1 copy.18
  145.0 0.1 convert_bitcast_fusion
  145.1 0.9 reshape.56
  (35 shorter events, 0.4 us)
Async XLA Ops:
  7.2 1.6 %copy-start = (bf16[1024,1024]{1,0:T(8,128)(2,1)S(1)}, bf16[1024,1024]{1,0:T(8,128)(2,1)}, u32[]{:S(2)}) copy-start(bf16[1024,1024]{1,0:T(8,128)(2,1)} %param.15) | copy-start | bytes 6291460
  7.2 3.3 %copy-start.10 = (bf16[1,1024,128]{2,1,0:T(8,128)(2,1)S(1)}, bf16[1,1024,128]{2,1,0:T(8,128)(2,1)}, u32[]{:S(2)}) copy-start(bf16[1,1024,128]{2,1,0:T(8,128)(2,1)} %param.12) | copy-start | bytes 786436
  7.2 3.3 %copy-start.11 = (bf16[1,1024,128]{2,1,0:T(8,128)(2,1)S(1)}, bf16[1,1024,128]{2,1,0:T(8,128)(2,1)}, u32[]{:S(2)}) copy-start(bf16[1,1024,128]{2,1,0:T(8,128)(2,1)} %param.11) | copy-start | bytes 786436
  7.2 3.3 %copy-start.12 = (bf16[1,1024,128]{2,1,0:T(8,128)(2,1)S(1)}, bf16[1,1024,128]{2,1,0:T(8,128)(2,1)}, u32[]{:S(2)}) copy-start(bf16[1,1024,128]{2,1,0:T(8,128)(2,1)} %param.10) | copy-start | bytes 786436
  7.2 88.8 %all-gather.3.cloned.1.call-start = ((), (), s32[]{:S(2)}) async-start(), calls=%async_computation.4 | async-start | bytes 4718592 | tf_op jit(solution)/shard_map/all_gather | solution.py:384
  10.5 1.3 copy-start.8
  10.5 1.3 copy-start.9
  12.6 47.0 %all-to-all-start = ((bf16[32,128,128]{2,1,0:T(8,128)(2,1)}), bf16[32,128,128]{2,1,0:T(8,128)(2,1)}, u32[]{:S(2)}, u32[]{:S(2)}) async-start(bf16[32,128,128]{2,1,0:T(8,128)(2,1)} %bitcast.6), calls=%async_computation | async-start | bytes 2097152 | tf_op jit(solution)/shard_map/all_to_all | solution.py:382
  24.7 121.3 %reduce-scatter.2.cloned.1.call-start = ((), (), s32[]{:S(2)}) async-start(), calls=%async_computation.3 | async-start | bytes 2359296 | tf_op jit(solution)/shard_map/reduce_scatter | solution.py:390
  26.1 3.0 %copy-start.2 = (bf16[1024,3072]{1,0:T(8,128)(2,1)S(1)}, bf16[1024,3072]{1,0:T(8,128)(2,1)}, u32[]{:S(2)}) copy-start(bf16[1024,3072]{1,0:T(8,128)(2,1)} %w_ref.1) | copy-start | bytes 18874372
  80.3 7.9 %collective-permute-start = (bf16[8,128,128]{2,1,0:T(8,128)(2,1)S(1)}, bf16[8,128,128]{2,1,0:T(8,128)(2,1)S(1)}, u32[]{:S(2)}, u32[]{:S(2)}) collective-permute-start(bf16[8,128,128]{2,1,0:T(8,128)(2,1)S(1)} %get-tuple-element.18), channel_id=1, source_target_pairs={{0,8},{8,16},{16,24},{24,0},{1,9},{9,17},{17,25},{25,1},{2,10},{10... | collective-permute-start | bytes 786440 | tf_op jit(solution)/shard_map/ppermute | solution.py:327
  83.1 10.2 %collective-permute-start.1 = (bf16[8,128,128]{2,1,0:T(8,128)(2,1)S(1)}, bf16[8,128,128]{2,1,0:T(8,128)(2,1)S(1)}, u32[]{:S(2)}, u32[]{:S(2)}) collective-permute-start(bf16[8,128,128]{2,1,0:T(8,128)(2,1)S(1)} %get-tuple-element.19), channel_id=1, source_target_pairs={{0,16},{8,24},{16,0},{24,8},{1,17},{9,25},{17,1},{25,9},{2,18},{10... | collective-permute-start | bytes 786440 | tf_op jit(solution)/shard_map/ppermute | solution.py:327
  85.2 8.1 %collective-permute-start.2 = (bf16[8,128,128]{2,1,0:T(8,128)(2,1)S(1)}, bf16[8,128,128]{2,1,0:T(8,128)(2,1)S(1)}, u32[]{:S(2)}, u32[]{:S(2)}) collective-permute-start(bf16[8,128,128]{2,1,0:T(8,128)(2,1)S(1)} %get-tuple-element.20), channel_id=1, source_target_pairs={{0,24},{8,0},{16,8},{24,16},{1,25},{9,1},{17,9},{25,17},{2,26},{10... | collective-permute-start | bytes 786440 | tf_op jit(solution)/shard_map/ppermute | solution.py:327
  93.3 1.3 copy-start.4
  93.3 1.3 copy-start.6
  94.5 1.4 copy-start.1
  95.9 0.9 copy-start.5
  95.9 1.0 copy-start.7
  96.9 2.2 %copy-start.3 = (bf16[16384,128]{1,0:T(8,128)(2,1)S(1)}, bf16[16384,128]{1,0:T(8,128)(2,1)}, u32[]{:S(2)}) copy-start(bf16[16384,128]{1,0:T(8,128)(2,1)} %all-gather.3.cloned.1.call-done) | copy-start | bytes 12582916
  101.2 6.4 %collective-permute-start.3 = (bf16[4,512,128]{2,1,0:T(8,128)(2,1)S(1)}, bf16[4,512,128]{2,1,0:T(8,128)(2,1)S(1)}, u32[]{:S(2)}, u32[]{:S(2)}) collective-permute-start(bf16[4,512,128]{2,1,0:T(8,128)(2,1)S(1)} %get-tuple-element.24), channel_id=1, source_target_pairs={{0,32},{32,0},{1,33},{33,1},{2,34},{34,2},{3,35},{35,3},{4,36},{36... | collective-permute-start | bytes 1572872 | tf_op jit(solution)/shard_map/ppermute | solution.py:322
  107.8 5.1 %collective-permute-start.6 = (bf16[512,128]{1,0:T(8,128)(2,1)S(1)}, bf16[512,128]{1,0:T(8,128)(2,1)S(1)}, u32[]{:S(2)}, u32[]{:S(2)}) collective-permute-start(bf16[512,128]{1,0:T(8,128)(2,1)S(1)} %get-tuple-element.28), channel_id=1, source_target_pairs={{0,24},{8,0},{16,8},{24,16},{1,25},{9,1},{17,9},{25,17},{2,26},{10... | collective-permute-start | bytes 393224 | tf_op jit(solution)/shard_map/ppermute | solution.py:327
  110.0 6.6 %collective-permute-start.5 = (bf16[512,128]{1,0:T(8,128)(2,1)S(1)}, bf16[512,128]{1,0:T(8,128)(2,1)S(1)}, u32[]{:S(2)}, u32[]{:S(2)}) collective-permute-start(bf16[512,128]{1,0:T(8,128)(2,1)S(1)} %get-tuple-element.29), channel_id=1, source_target_pairs={{0,8},{8,16},{16,24},{24,0},{1,9},{9,17},{17,25},{25,1},{2,10},{10... | collective-permute-start | bytes 393224 | tf_op jit(solution)/shard_map/ppermute | solution.py:327
  110.0 7.6 %collective-permute-start.4 = (bf16[512,128]{1,0:T(8,128)(2,1)S(1)}, bf16[512,128]{1,0:T(8,128)(2,1)S(1)}, u32[]{:S(2)}, u32[]{:S(2)}) collective-permute-start(bf16[512,128]{1,0:T(8,128)(2,1)S(1)} %get-tuple-element.27), channel_id=1, source_target_pairs={{0,16},{8,24},{16,0},{24,8},{1,17},{9,25},{17,1},{25,9},{2,18},{10... | collective-permute-start | bytes 393224 | tf_op jit(solution)/shard_map/ppermute | solution.py:327
  117.7 4.3 %collective-permute-start.7 = (bf16[512,128]{1,0:T(8,128)(2,1)S(1)}, bf16[512,128]{1,0:T(8,128)(2,1)S(1)}, u32[]{:S(2)}, u32[]{:S(2)}) collective-permute-start(bf16[512,128]{1,0:T(8,128)(2,1)S(1)} %fusion.1), channel_id=1, source_target_pairs={{0,64},{64,0},{128,192},{192,128},{1,65},{65,1},{129,193},{193,129... | collective-permute-start | bytes 393224 | tf_op jit(solution)/shard_map/ppermute | solution.py:338
  122.0 5.6 %collective-permute-start.8 = (bf16[512,128]{1,0:T(8,128)(2,1)S(1)}, bf16[512,128]{1,0:T(8,128)(2,1)S(1)}, u32[]{:S(2)}, u32[]{:S(2)}) collective-permute-start(bf16[512,128]{1,0:T(8,128)(2,1)S(1)} %add_convert_fusion.2), channel_id=1, source_target_pairs={{0,192},{192,0},{64,128},{128,64},{1,193},{193,1},{65,129},{129,65... | collective-permute-start | bytes 393224 | tf_op jit(solution)/shard_map/ppermute | solution.py:339
  127.6 7.9 %collective-permute-start.9 = (bf16[384,128]{1,0:T(8,128)(2,1)S(1)}, bf16[384,128]{1,0:T(8,128)(2,1)S(1)}, u32[]{:S(2)}, u32[]{:S(2)}) collective-permute-start(bf16[384,128]{1,0:T(8,128)(2,1)S(1)} %slice.29), channel_id=1, source_target_pairs={{0,32},{32,0},{1,33},{33,1},{2,34},{34,2},{3,35},{35,3},{4,36},{36... | collective-permute-start | bytes 294920 | tf_op jit(solution)/shard_map/ppermute | solution.py:322
  132.1 10.3 %all-to-all-start.1 = ((bf16[8,16,128]{2,1,0:T(8,128)(2,1)}), bf16[8,16,128]{2,1,0:T(8,128)(2,1)S(1)}, u32[]{:S(2)}, u32[]{:S(2)}) async-start(bf16[8,16,128]{2,1,0:T(8,128)(2,1)} %bitcast.19), calls=%async_computation.2 | async-start | bytes 65536 | tf_op jit(solution)/shard_map/all_to_all | solution.py:355
  142.4 2.4 %collective-permute-start.10 = (bf16[8,16,128]{2,1,0:T(8,128)(2,1)S(1)}, bf16[8,16,128]{2,1,0:T(8,128)(2,1)S(1)}, u32[]{:S(2)}, u32[]{:S(2)}) collective-permute-start(bf16[8,16,128]{2,1,0:T(8,128)(2,1)S(1)} %all-to-all-done.1), channel_id=1, source_target_pairs={{0,32},{32,0},{1,33},{33,1},{2,34},{34,2},{3,35},{35,3},{4,36},{36... | collective-permute-start | bytes 98312 | tf_op jit(solution)/shard_map/ppermute | solution.py:322
Sparse Core Ops, SparseCore 0:
  12.8 77.9 all-gather.2
  96.1 39.4 reduce-scatter.1

commit v5 on v4

--- a/solution.py
+++ b/solution.py
@@ -335,8 +335,7 @@
 
 
 def sum_over_y(v):
-    v = add_up(v, lax.ppermute(v, "y", [(0, 1), (1, 0), (2, 3), (3, 2)]))
-    return add_up(v, lax.ppermute(v, "y", [(0, 3), (3, 0), (1, 2), (2, 1)]))
+    return add_up(v, shift(v, "y", 2), shift(v, "y", 1), shift(v, "y", 3))
 
 
 def weight_grads(mine, other, width):

time: 153 us -> 153 us (level)
    ppermute x2 -> x0, waiting for transfers between devices: 5.24 us -> none  [the longest x1 2.88 us: sum_over_y(): v = add_up(v, lax.ppermute(v, 'y', [(0, 1), (1, 0), (2, 3), (3, 2)]))]
    ppermute x6 -> x9, waiting for transfers between devices: 12.8 us -> 17.8 us  [shift(): return lax.ppermute(v, axis, [(i, (i + k) % n) for i in range(n)])]
    ppermute x6 -> x9, starting transfers between devices: 9.95 us -> 14.7 us  [shift(): return lax.ppermute(v, axis, [(i, (i + k) % n) for i in range(n)])]
    ppermute x2 -> x0, starting transfers between devices: 4.63 us -> none  [the longest x1 3.21 us: sum_over_y(): return add_up(v, lax.ppermute(v, 'y', [(0, 3), (3, 0), (1, 2), (2, 1)]))]
  transfers between devices with their start and end apart: 15 -> 16, of which waited for: 11 -> 11; matrix products, arithmetic and copies ran while one was open for 2% -> 2% of each run, Pallas kernels for 17% -> 17%
where the time goes in v5:
time: 153 us
  waiting for transfers between devices  54.4 us (36%)
  starting transfers between devices  40.7 us (27%)
  Pallas kernels  25.9 us (17%)
  between operations  15.6 us (10%)
  local copies, waits for them, and re-layouts  13.3 us (9%)
  matrix products  1.71 us (1%)
    all_to_all x1, waiting for transfers between devices, body(): heads = lax.all_to_all(sent, ('z', 'x'), 0, 0, tiled=True)  28.7 us
    pallas_call x4, Pallas kernels, kernel_call(): pl.pallas_call(kernel, out_shape=outs, in_specs=[pl.BlockSpec(memory_spac...  25.9 us
    ppermute x9, waiting for transfers between devices, shift(): return lax.ppermute(v, axis, [(i, (i + k) % n) for i in range(n)])  17.8 us
    ppermute x9, starting transfers between devices, shift(): return lax.ppermute(v, axis, [(i, (i + k) % n) for i in range(n)])  14.7 us
    all_to_all x1, starting transfers between devices, body(): heads = lax.all_to_all(sent, ('z', 'x'), 0, 0, tiled=True)  12 us
    ppermute x3, starting transfers between devices, swap_cores(): return lax.ppermute(v, 'core', [(0, 1), (1, 0)])  9.87 us
    unnamed x26, local copies, waits for them, and re-layouts  9.04 us
    all_to_all x1, waiting for transfers between devices, weight_grads(): out = lax.all_to_all(out, 'z', 0, 0, tiled=True)  5.62 us
  transfers between devices with their start and end apart: 16, of which 11 were waited for; matrix products, arithmetic and copies ran while one was open for 2% of the time, Pallas kernels for 17%

profile of v5, /device:TPU:1, one launch (start us, length us, event | category | flops | bytes accessed | tf_op | source)
XLA Modules:
  0.0 153.0 jit_solution(7991160849500922131)
XLA Ops:
  7.3 1.5 copy-done
  8.8 1.7 %convolution_convert_fusion = bf16[1024,128]{1,0:T(8,128)(2,1)S(1)} fusion(bf16[1024,1024]{1,0:T(8,128)(2,1)S(1)} %copy-done, bf16[1,1024,128]{2,1,0:T(8,128)(2,1)} %param.13), kind=kOutput, calls=%fused_computation | convolution fusion | flops 268566528 | bytes 2621440 | tf_op jit(solution)/shard_map/dot_general | solution.py:373
  10.5 0.1 pad_maximum_fusion
  10.7 1.1 copy.21
  11.8 0.8 pad_maximum_fusion.1
  12.6 12.0 %all-to-all-start = ((bf16[32,128,128]{2,1,0:T(8,128)(2,1)}), bf16[32,128,128]{2,1,0:T(8,128)(2,1)}, u32[]{:S(2)}, u32[]{:S(2)}) async-start(bf16[32,128,128]{2,1,0:T(8,128)(2,1)} %bitcast.6), calls=%async_computation | async-start | bytes 2097152 | tf_op jit(solution)/shard_map/all_to_all | solution.py:381
  26.0 0.1 pad_add_fusion.ids_ref
  26.1 3.0 %copy-done.2 = bf16[1024,3072]{1,0:T(8,128)(2,1)S(1)} copy-done((bf16[1024,3072]{1,0:T(8,128)(2,1)S(1)}, bf16[1024,3072]{1,0:T(8,128)(2,1)}, u32[]{:S(2)}) %copy-start.2) | copy-done | bytes 6291480
  29.1 1.9 %own_weights.1.weights_ref = bf16[1024,384]{1,0:T(8,128)(2,1)S(1)} custom-call(s32[4]{0:T(128)S(1)} %pad_add_fusion.ids_ref, bf16[1024,3072]{1,0:T(8,128)(2,1)S(1)} %copy-done.2), custom_call_target="tpu_custom_call" | custom-call | bytes 7077904 | tf_op jit(solution)/shard_map/own_weights/pallas_call | solution.py:170
  30.9 28.7 %all-to-all-done.x_ref = bf16[32,128,128]{2,1,0:T(8,128)(2,1)} async-done(((bf16[32,128,128]{2,1,0:T(8,128)(2,1)}), bf16[32,128,128]{2,1,0:T(8,128)(2,1)}, u32[]{:S(2)}, u32[]{:S(2)}) %all-to-all-start) | async-done | bytes 1048608 | tf_op jit(solution)/shard_map/all_to_all | solution.py:381
  59.6 20.6 %window_attention.1 = (bf16[8,128,128]{2,1,0:T(8,128)(2,1)S(1)}, bf16[8,128,128]{2,1,0:T(8,128)(2,1)S(1)}, bf16[8,128,128]{2,1,0:T(8,128)(2,1)S(1)}, bf16[8,128,128]{2,1,0:T(8,128)(2,1)S(1)}) custom-call(s32[4]{0:T(128)S(1)} %pad_add_fusion.ids_ref, bf16[32,128,128]{2,1,0:T(8,128)(2,1)} %all-to-all-done.x_ref), custom_call_target="tpu_custom_call" | custom-call | flops 2013265920 | bytes 2097168 | tf_op jit(solution)/shard_map/window_attention/pallas_call | solution.py:170
  80.3 2.8 %collective-permute-start = (bf16[8,128,128]{2,1,0:T(8,128)(2,1)S(1)}, bf16[8,128,128]{2,1,0:T(8,128)(2,1)S(1)}, u32[]{:S(2)}, u32[]{:S(2)}) collective-permute-start(bf16[8,128,128]{2,1,0:T(8,128)(2,1)S(1)} %get-tuple-element.18), channel_id=1, source_target_pairs={{0,8},{8,16},{16,24},{24,0},{1,9},{9,17},{17,25},{25,1},{2,10},{10... | collective-permute-start | bytes 786440 | tf_op jit(solution)/shard_map/ppermute | solution.py:327
  83.1 2.1 %collective-permute-start.1 = (bf16[8,128,128]{2,1,0:T(8,128)(2,1)S(1)}, bf16[8,128,128]{2,1,0:T(8,128)(2,1)S(1)}, u32[]{:S(2)}, u32[]{:S(2)}) collective-permute-start(bf16[8,128,128]{2,1,0:T(8,128)(2,1)S(1)} %get-tuple-element.19), channel_id=1, source_target_pairs={{0,16},{8,24},{16,0},{24,8},{1,17},{9,25},{17,1},{25,9},{2,18},{10... | collective-permute-start | bytes 786440 | tf_op jit(solution)/shard_map/ppermute | solution.py:327
  85.2 1.0 collective-permute-start.2
  86.2 2.0 %collective-permute-done.refs_1_ = bf16[8,128,128]{2,1,0:T(8,128)(2,1)S(1)} collective-permute-done((bf16[8,128,128]{2,1,0:T(8,128)(2,1)S(1)}, bf16[8,128,128]{2,1,0:T(8,128)(2,1)S(1)}, u32[]{:S(2)}, u32[]{:S(2)}) %collective-permute-start) | collective-permute-done | bytes 262176 | tf_op jit(solution)/shard_map/ppermute | solution.py:327
  88.2 5.1 %collective-permute-done.1.refs_2_ = bf16[8,128,128]{2,1,0:T(8,128)(2,1)S(1)} collective-permute-done((bf16[8,128,128]{2,1,0:T(8,128)(2,1)S(1)}, bf16[8,128,128]{2,1,0:T(8,128)(2,1)S(1)}, u32[]{:S(2)}, u32[]{:S(2)}) %collective-permute-start.1) | collective-permute-done | bytes 262176 | tf_op jit(solution)/shard_map/ppermute | solution.py:327
  93.3 1.2 input_terms.1
  94.5 1.4 copy-done.1
  96.0 0.9 copy-done.5
  96.9 0.1 copy-done.7
  96.9 2.2 %copy-done.3 = bf16[16384,128]{1,0:T(8,128)(2,1)S(1)} copy-done((bf16[16384,128]{1,0:T(8,128)(2,1)S(1)}, bf16[16384,128]{1,0:T(8,128)(2,1)}, u32[]{:S(2)}) %copy-start.3) | copy-done | bytes 4194328
  99.1 2.1 %weight_grad_terms.1 = (bf16[4,512,128]{2,1,0:T(8,128)(2,1)S(1)}, bf16[4,512,128]{2,1,0:T(8,128)(2,1)S(1)}) custom-call(s32[4]{0:T(128)S(1)} %pad_add_fusion.ids_ref, bf16[8,128,128]{2,1,0:T(8,128)(2,1)S(1)} %get-tuple-element.17.refs_0_, bf16[8,128,128]{2,1,0:T(8,128)(2,1)S(1)} %collective-permute-done.refs_1_, bf16[8,128,128]{2,1,0:T(8,128)(2,1)S(1)} %copy-done.5, ...), custom_call_target="tpu_custom_call" | custom-call | flops 1073741824 | bytes 6291472 | tf_op jit(solution)/shard_map/weight_grad_terms/pallas_call | solution.py:170
  101.2 4.9 %collective-permute-start.3 = (bf16[4,512,128]{2,1,0:T(8,128)(2,1)S(1)}, bf16[4,512,128]{2,1,0:T(8,128)(2,1)S(1)}, u32[]{:S(2)}, u32[]{:S(2)}) collective-permute-start(bf16[4,512,128]{2,1,0:T(8,128)(2,1)S(1)} %get-tuple-element.24), channel_id=1, source_target_pairs={{0,32},{32,0},{1,33},{33,1},{2,34},{34,2},{3,35},{35,3},{4,36},{36... | collective-permute-start | bytes 1572872 | tf_op jit(solution)/shard_map/ppermute | solution.py:322
  106.1 1.5 %collective-permute-done.3 = bf16[4,512,128]{2,1,0:T(8,128)(2,1)S(1)} collective-permute-done((bf16[4,512,128]{2,1,0:T(8,128)(2,1)S(1)}, bf16[4,512,128]{2,1,0:T(8,128)(2,1)S(1)}, u32[]{:S(2)}, u32[]{:S(2)}) %collective-permute-start.3) | collective-permute-done | bytes 524320 | tf_op jit(solution)/shard_map/ppermute | solution.py:322
  107.7 0.1 add_convert_fusion
  107.8 2.1 %collective-permute-start.6 = (bf16[512,128]{1,0:T(8,128)(2,1)S(1)}, bf16[512,128]{1,0:T(8,128)(2,1)S(1)}, u32[]{:S(2)}, u32[]{:S(2)}) collective-permute-start(bf16[512,128]{1,0:T(8,128)(2,1)S(1)} %get-tuple-element.28), channel_id=1, source_target_pairs={{0,24},{8,0},{16,8},{24,16},{1,25},{9,1},{17,9},{25,17},{2,26},{10... | collective-permute-start | bytes 393224 | tf_op jit(solution)/shard_map/ppermute | solution.py:327
  110.0 1.9 %collective-permute-start.4 = (bf16[512,128]{1,0:T(8,128)(2,1)S(1)}, bf16[512,128]{1,0:T(8,128)(2,1)S(1)}, u32[]{:S(2)}, u32[]{:S(2)}) collective-permute-start(bf16[512,128]{1,0:T(8,128)(2,1)S(1)} %get-tuple-element.27), channel_id=1, source_target_pairs={{0,16},{8,24},{16,0},{24,8},{1,17},{9,25},{17,1},{25,9},{2,18},{10... | collective-permute-start | bytes 393224 | tf_op jit(solution)/shard_map/ppermute | solution.py:327
  111.9 1.1 collective-permute-done.6
  112.9 3.7 %collective-permute-done.5 = bf16[512,128]{1,0:T(8,128)(2,1)S(1)} collective-permute-done((bf16[512,128]{1,0:T(8,128)(2,1)S(1)}, bf16[512,128]{1,0:T(8,128)(2,1)S(1)}, u32[]{:S(2)}, u32[]{:S(2)}) %collective-permute-start.5) | collective-permute-done | bytes 131104 | tf_op jit(solution)/shard_map/ppermute | solution.py:327
  116.6 1.0 collective-permute-done.4
  117.7 3.2 %collective-permute-start.9 = (bf16[512,128]{1,0:T(8,128)(2,1)S(1)}, bf16[512,128]{1,0:T(8,128)(2,1)S(1)}, u32[]{:S(2)}, u32[]{:S(2)}) collective-permute-start(bf16[512,128]{1,0:T(8,128)(2,1)S(1)} %fusion.1), channel_id=1, source_target_pairs={{0,192},{64,0},{128,64},{192,128},{1,193},{65,1},{129,65},{193,129... | collective-permute-start | bytes 393224 | tf_op jit(solution)/shard_map/ppermute | solution.py:327
  120.9 1.5 collective-permute-start.7
  122.4 0.4 collective-permute-done.9
  122.8 4.6 %collective-permute-done.8 = bf16[512,128]{1,0:T(8,128)(2,1)S(1)} collective-permute-done((bf16[512,128]{1,0:T(8,128)(2,1)S(1)}, bf16[512,128]{1,0:T(8,128)(2,1)S(1)}, u32[]{:S(2)}, u32[]{:S(2)}) %collective-permute-start.8) | collective-permute-done | bytes 131104 | tf_op jit(solution)/shard_map/ppermute | solution.py:327
  127.6 3.5 %collective-permute-start.10 = (bf16[384,128]{1,0:T(8,128)(2,1)S(1)}, bf16[384,128]{1,0:T(8,128)(2,1)S(1)}, u32[]{:S(2)}, u32[]{:S(2)}) collective-permute-start(bf16[384,128]{1,0:T(8,128)(2,1)S(1)} %slice.29), channel_id=1, source_target_pairs={{0,32},{32,0},{1,33},{33,1},{2,34},{34,2},{3,35},{35,3},{4,36},{36... | collective-permute-start | bytes 294920 | tf_op jit(solution)/shard_map/ppermute | solution.py:322
  131.0 0.6 slice.28
  131.7 4.1 %all-to-all-start.1 = ((bf16[8,16,128]{2,1,0:T(8,128)(2,1)}), bf16[8,16,128]{2,1,0:T(8,128)(2,1)S(1)}, u32[]{:S(2)}, u32[]{:S(2)}) async-start(bf16[8,16,128]{2,1,0:T(8,128)(2,1)} %bitcast.19), calls=%async_computation.2 | async-start | bytes 65536 | tf_op jit(solution)/shard_map/all_to_all | solution.py:354
  135.8 0.3 copy.16
  136.0 0.9 reshape.55
  136.9 5.6 %all-to-all-done.1 = bf16[8,16,128]{2,1,0:T(8,128)(2,1)S(1)} async-done(((bf16[8,16,128]{2,1,0:T(8,128)(2,1)}), bf16[8,16,128]{2,1,0:T(8,128)(2,1)S(1)}, u32[]{:S(2)}, u32[]{:S(2)}) %all-to-all-start.1) | async-done | bytes 32800 | tf_op jit(solution)/shard_map/all_to_all | solution.py:354
  142.5 1.5 collective-permute-start.11
  144.0 0.1 stack.49
  144.2 0.1 copy.17
  144.3 0.6 collective-permute-done.11
  144.9 0.1 stack.50
  145.0 0.1 copy.18
  145.1 0.1 convert_bitcast_fusion
  145.2 0.9 reshape.56
  (36 shorter events, 0.4 us)
Async XLA Ops:
  7.2 1.6 %copy-start = (bf16[1024,1024]{1,0:T(8,128)(2,1)S(1)}, bf16[1024,1024]{1,0:T(8,128)(2,1)}, u32[]{:S(2)}) copy-start(bf16[1024,1024]{1,0:T(8,128)(2,1)} %param.15) | copy-start | bytes 6291460
  7.2 3.3 %copy-start.10 = (bf16[1,1024,128]{2,1,0:T(8,128)(2,1)S(1)}, bf16[1,1024,128]{2,1,0:T(8,128)(2,1)}, u32[]{:S(2)}) copy-start(bf16[1,1024,128]{2,1,0:T(8,128)(2,1)} %param.12) | copy-start | bytes 786436
  7.2 3.3 %copy-start.11 = (bf16[1,1024,128]{2,1,0:T(8,128)(2,1)S(1)}, bf16[1,1024,128]{2,1,0:T(8,128)(2,1)}, u32[]{:S(2)}) copy-start(bf16[1,1024,128]{2,1,0:T(8,128)(2,1)} %param.11) | copy-start | bytes 786436
  7.2 3.3 %copy-start.12 = (bf16[1,1024,128]{2,1,0:T(8,128)(2,1)S(1)}, bf16[1,1024,128]{2,1,0:T(8,128)(2,1)}, u32[]{:S(2)}) copy-start(bf16[1,1024,128]{2,1,0:T(8,128)(2,1)} %param.10) | copy-start | bytes 786436
  7.2 88.8 %all-gather.3.cloned.1.call-start = ((), (), s32[]{:S(2)}) async-start(), calls=%async_computation.4 | async-start | bytes 4718592 | tf_op jit(solution)/shard_map/all_gather | solution.py:383
  10.5 1.3 copy-start.8
  10.5 1.3 copy-start.9
  12.6 47.0 %all-to-all-start = ((bf16[32,128,128]{2,1,0:T(8,128)(2,1)}), bf16[32,128,128]{2,1,0:T(8,128)(2,1)}, u32[]{:S(2)}, u32[]{:S(2)}) async-start(bf16[32,128,128]{2,1,0:T(8,128)(2,1)} %bitcast.6), calls=%async_computation | async-start | bytes 2097152 | tf_op jit(solution)/shard_map/all_to_all | solution.py:381
  24.7 121.5 %reduce-scatter.2.cloned.1.call-start = ((), (), s32[]{:S(2)}) async-start(), calls=%async_computation.3 | async-start | bytes 2359296 | tf_op jit(solution)/shard_map/reduce_scatter | solution.py:389
  26.1 3.0 %copy-start.2 = (bf16[1024,3072]{1,0:T(8,128)(2,1)S(1)}, bf16[1024,3072]{1,0:T(8,128)(2,1)}, u32[]{:S(2)}) copy-start(bf16[1024,3072]{1,0:T(8,128)(2,1)} %w_ref.1) | copy-start | bytes 18874372
  80.3 7.9 %collective-permute-start = (bf16[8,128,128]{2,1,0:T(8,128)(2,1)S(1)}, bf16[8,128,128]{2,1,0:T(8,128)(2,1)S(1)}, u32[]{:S(2)}, u32[]{:S(2)}) collective-permute-start(bf16[8,128,128]{2,1,0:T(8,128)(2,1)S(1)} %get-tuple-element.18), channel_id=1, source_target_pairs={{0,8},{8,16},{16,24},{24,0},{1,9},{9,17},{17,25},{25,1},{2,10},{10... | collective-permute-start | bytes 786440 | tf_op jit(solution)/shard_map/ppermute | solution.py:327
  83.1 10.2 %collective-permute-start.1 = (bf16[8,128,128]{2,1,0:T(8,128)(2,1)S(1)}, bf16[8,128,128]{2,1,0:T(8,128)(2,1)S(1)}, u32[]{:S(2)}, u32[]{:S(2)}) collective-permute-start(bf16[8,128,128]{2,1,0:T(8,128)(2,1)S(1)} %get-tuple-element.19), channel_id=1, source_target_pairs={{0,16},{8,24},{16,0},{24,8},{1,17},{9,25},{17,1},{25,9},{2,18},{10... | collective-permute-start | bytes 786440 | tf_op jit(solution)/shard_map/ppermute | solution.py:327
  85.2 8.1 %collective-permute-start.2 = (bf16[8,128,128]{2,1,0:T(8,128)(2,1)S(1)}, bf16[8,128,128]{2,1,0:T(8,128)(2,1)S(1)}, u32[]{:S(2)}, u32[]{:S(2)}) collective-permute-start(bf16[8,128,128]{2,1,0:T(8,128)(2,1)S(1)} %get-tuple-element.20), channel_id=1, source_target_pairs={{0,24},{8,0},{16,8},{24,16},{1,25},{9,1},{17,9},{25,17},{2,26},{10... | collective-permute-start | bytes 786440 | tf_op jit(solution)/shard_map/ppermute | solution.py:327
  93.3 1.3 copy-start.4
  93.3 1.3 copy-start.6
  94.5 1.4 copy-start.1
  95.9 0.9 copy-start.5
  95.9 1.0 copy-start.7
  96.9 2.2 %copy-start.3 = (bf16[16384,128]{1,0:T(8,128)(2,1)S(1)}, bf16[16384,128]{1,0:T(8,128)(2,1)}, u32[]{:S(2)}) copy-start(bf16[16384,128]{1,0:T(8,128)(2,1)} %all-gather.3.cloned.1.call-done) | copy-start | bytes 12582916
  101.2 6.4 %collective-permute-start.3 = (bf16[4,512,128]{2,1,0:T(8,128)(2,1)S(1)}, bf16[4,512,128]{2,1,0:T(8,128)(2,1)S(1)}, u32[]{:S(2)}, u32[]{:S(2)}) collective-permute-start(bf16[4,512,128]{2,1,0:T(8,128)(2,1)S(1)} %get-tuple-element.24), channel_id=1, source_target_pairs={{0,32},{32,0},{1,33},{33,1},{2,34},{34,2},{3,35},{35,3},{4,36},{36... | collective-permute-start | bytes 1572872 | tf_op jit(solution)/shard_map/ppermute | solution.py:322
  107.8 5.1 %collective-permute-start.6 = (bf16[512,128]{1,0:T(8,128)(2,1)S(1)}, bf16[512,128]{1,0:T(8,128)(2,1)S(1)}, u32[]{:S(2)}, u32[]{:S(2)}) collective-permute-start(bf16[512,128]{1,0:T(8,128)(2,1)S(1)} %get-tuple-element.28), channel_id=1, source_target_pairs={{0,24},{8,0},{16,8},{24,16},{1,25},{9,1},{17,9},{25,17},{2,26},{10... | collective-permute-start | bytes 393224 | tf_op jit(solution)/shard_map/ppermute | solution.py:327
  110.0 6.6 %collective-permute-start.5 = (bf16[512,128]{1,0:T(8,128)(2,1)S(1)}, bf16[512,128]{1,0:T(8,128)(2,1)S(1)}, u32[]{:S(2)}, u32[]{:S(2)}) collective-permute-start(bf16[512,128]{1,0:T(8,128)(2,1)S(1)} %get-tuple-element.29), channel_id=1, source_target_pairs={{0,8},{8,16},{16,24},{24,0},{1,9},{9,17},{17,25},{25,1},{2,10},{10... | collective-permute-start | bytes 393224 | tf_op jit(solution)/shard_map/ppermute | solution.py:327
  110.0 7.6 %collective-permute-start.4 = (bf16[512,128]{1,0:T(8,128)(2,1)S(1)}, bf16[512,128]{1,0:T(8,128)(2,1)S(1)}, u32[]{:S(2)}, u32[]{:S(2)}) collective-permute-start(bf16[512,128]{1,0:T(8,128)(2,1)S(1)} %get-tuple-element.27), channel_id=1, source_target_pairs={{0,16},{8,24},{16,0},{24,8},{1,17},{9,25},{17,1},{25,9},{2,18},{10... | collective-permute-start | bytes 393224 | tf_op jit(solution)/shard_map/ppermute | solution.py:327
  117.7 5.2 %collective-permute-start.9 = (bf16[512,128]{1,0:T(8,128)(2,1)S(1)}, bf16[512,128]{1,0:T(8,128)(2,1)S(1)}, u32[]{:S(2)}, u32[]{:S(2)}) collective-permute-start(bf16[512,128]{1,0:T(8,128)(2,1)S(1)} %fusion.1), channel_id=1, source_target_pairs={{0,192},{64,0},{128,64},{192,128},{1,193},{65,1},{129,65},{193,129... | collective-permute-start | bytes 393224 | tf_op jit(solution)/shard_map/ppermute | solution.py:327
  120.9 6.6 %collective-permute-start.8 = (bf16[512,128]{1,0:T(8,128)(2,1)S(1)}, bf16[512,128]{1,0:T(8,128)(2,1)S(1)}, u32[]{:S(2)}, u32[]{:S(2)}) collective-permute-start(bf16[512,128]{1,0:T(8,128)(2,1)S(1)} %fusion.1), channel_id=1, source_target_pairs={{0,64},{64,128},{128,192},{192,0},{1,65},{65,129},{129,193},{193,1... | collective-permute-start | bytes 393224 | tf_op jit(solution)/shard_map/ppermute | solution.py:327
  120.9 6.6 %collective-permute-start.7 = (bf16[512,128]{1,0:T(8,128)(2,1)S(1)}, bf16[512,128]{1,0:T(8,128)(2,1)S(1)}, u32[]{:S(2)}, u32[]{:S(2)}) collective-permute-start(bf16[512,128]{1,0:T(8,128)(2,1)S(1)} %fusion.1), channel_id=1, source_target_pairs={{0,128},{64,192},{128,0},{192,64},{1,129},{65,193},{129,1},{193,65... | collective-permute-start | bytes 393224 | tf_op jit(solution)/shard_map/ppermute | solution.py:327
  127.6 8.2 %collective-permute-start.10 = (bf16[384,128]{1,0:T(8,128)(2,1)S(1)}, bf16[384,128]{1,0:T(8,128)(2,1)S(1)}, u32[]{:S(2)}, u32[]{:S(2)}) collective-permute-start(bf16[384,128]{1,0:T(8,128)(2,1)S(1)} %slice.29), channel_id=1, source_target_pairs={{0,32},{32,0},{1,33},{33,1},{2,34},{34,2},{3,35},{35,3},{4,36},{36... | collective-permute-start | bytes 294920 | tf_op jit(solution)/shard_map/ppermute | solution.py:322
  131.7 10.9 %all-to-all-start.1 = ((bf16[8,16,128]{2,1,0:T(8,128)(2,1)}), bf16[8,16,128]{2,1,0:T(8,128)(2,1)S(1)}, u32[]{:S(2)}, u32[]{:S(2)}) async-start(bf16[8,16,128]{2,1,0:T(8,128)(2,1)} %bitcast.19), calls=%async_computation.2 | async-start | bytes 65536 | tf_op jit(solution)/shard_map/all_to_all | solution.py:354
  142.5 2.4 %collective-permute-start.11 = (bf16[8,16,128]{2,1,0:T(8,128)(2,1)S(1)}, bf16[8,16,128]{2,1,0:T(8,128)(2,1)S(1)}, u32[]{:S(2)}, u32[]{:S(2)}) collective-permute-start(bf16[8,16,128]{2,1,0:T(8,128)(2,1)S(1)} %all-to-all-done.1), channel_id=1, source_target_pairs={{0,32},{32,0},{1,33},{33,1},{2,34},{34,2},{3,35},{35,3},{4,36},{36... | collective-permute-start | bytes 98312 | tf_op jit(solution)/shard_map/ppermute | solution.py:322
Sparse Core Ops, SparseCore 0:
  12.8 77.9 all-gather.2
  96.1 39.4 reduce-scatter.1
